TPU v7x, 512 devices: a whole 4x4x16 slice. The times are simulated.
512 devices in a mesh: ctx: 32 (over z, core), tp: 16 (over x, y).
Axes of the slice: x: 4, y: 4, z: 16, core: 2. Of those that a mesh axis runs over, the one named last changes fastest.
Arguments:
- inputs: bfloat16 [4096, 4096], P('ctx'), may hold values from -6 to 6
- w_in: bfloat16 [4096, 4096], P('ctx', 'tp'), may hold values from -0.09375 to 0.09375
- b_in: bfloat16 [4096, 128], P('ctx'), may hold values from -0.25 to 0.25
- c_in: bfloat16 [4096, 128], P('ctx'), may hold values from -0.75 to 0.75
- log_decay: float32 [4096, 64], P('ctx', 'tp'), may hold values from -0.75 to 0, as said below
- skip: float32 [64], P('tp'), may hold values from 0.5 to 1.5
- d_out: bfloat16 [4096, 4096], P('ctx', 'tp'), may hold values from -0.0234375 to 0.0234375
Outputs:
- d_w: float32 [4096, 4096], P('ctx', 'tp')
- d_b: float32 [4096, 128], P('ctx')
- d_c: float32 [4096, 128], P('ctx')
Inputs may be any that keep to these rules, and one draw needn't show every extreme that they name: `log_decay`: never positive.
All inputs are finite; a program needn't handle non-finite values.
Results may differ from a plain program's by a relative error of at most 0.0034.
Values may be sent and summed in bfloat16 or wider, within the bound.
A program may use at most 64 MiB of HBM per device.

v0:
```python
import jax
import jax.numpy as jnp
from jax import lax
from jax.sharding import PartitionSpec as P


def carried_in(shard, axis, combine, identity, reverse):
    count, mine = (lax.axis_size(axis), lax.axis_index(axis))
    everything = jax.tree.map(lambda part: lax.all_gather(part, axis), shard)
    start = jax.tree.map(
        lambda part, zero: jnp.broadcast_to(jnp.asarray(zero, part.dtype), part.shape),
        shard,
        identity,
    )

    def step(k, before):
        at = count - 1 - k if reverse else k
        reached = at > mine if reverse else at < mine
        new = combine(before, jax.tree.map(lambda part: part[at], everything))
        return jax.tree.map(lambda a, b: jnp.where(reached, a, b), new, before)

    return lax.fori_loop(0, count, step, start)


def link_pairs(earlier, later):
    first_decay, first_state = earlier
    second_decay, second_state = later
    return (first_decay * second_decay, second_decay[:, None, None] * first_state + second_state)


def per_device(inputs, w_in, b_in, c_in, log_decay, skip, d_out):
    length = inputs.shape[0]
    heads_here = log_decay.shape[1]
    columns = w_in.shape[1]
    head_size = columns // heads_here
    state_size = b_in.shape[1]
    taken = inputs
    projected = jnp.dot(
        taken, lax.all_gather(w_in, "ctx", axis=0, tiled=True), preferred_element_type=jnp.float32
    )
    values = projected.astype(jnp.bfloat16)
    values_heads = values.reshape(length, heads_here, head_size)
    upstream = d_out.reshape(length, heads_here, head_size)
    cumulative = jnp.cumsum(log_decay, axis=0)
    block_log = cumulative[length - 1]
    block_decay = jnp.exp(block_log)
    to_end = jnp.exp(block_log[None, :] - cumulative)
    from_start = jnp.exp(cumulative)
    b_float = b_in.astype(jnp.float32)
    output_matrix_wide = c_in.astype(jnp.float32)
    values_float = values_heads.astype(jnp.float32)
    upstream_float = upstream.astype(jnp.float32)
    state_end = jnp.einsum(
        "lh,ln,lhp->hnp", to_end, b_float, values_float, precision=lax.Precision.HIGHEST
    )
    adjoint_start = jnp.einsum(
        "lh,ln,lhp->hnp",
        from_start,
        output_matrix_wide,
        upstream_float,
        precision=lax.Precision.HIGHEST,
    )
    zero_state = jnp.zeros((heads_here, state_size, head_size), jnp.float32)
    identity = (jnp.ones((heads_here,), jnp.float32), zero_state)
    state_in = carried_in((block_decay, state_end), "ctx", link_pairs, identity, False)[1]
    adjoint_in = carried_in((block_decay, adjoint_start), "ctx", link_pairs, identity, True)[1]
    positions = jnp.arange(length)
    causal = (positions[:, None] >= positions[None, :])[None]
    decay_rows = cumulative.T
    log_gap = decay_rows[:, :, None] - decay_rows[:, None, :]
    within = jnp.where(causal, jnp.exp(jnp.where(causal, log_gap, 0.0)), 0.0)
    scores = jnp.einsum("sn,tn->st", c_in, b_in, preferred_element_type=jnp.float32)
    mixing = (within * scores[None]).astype(jnp.bfloat16)
    grad_local = jnp.einsum("hst,shp->thp", mixing, upstream, preferred_element_type=jnp.float32)
    grad_carried = to_end[:, :, None] * jnp.einsum(
        "tn,hnp->thp", b_float, adjoint_in, precision=lax.Precision.HIGHEST
    )
    grad_values = (grad_local + grad_carried + skip[None, :, None] * upstream_float).astype(
        jnp.bfloat16
    )
    grad_values = grad_values.reshape(length, columns)
    gram = jnp.einsum("thp,shp->hts", upstream, values_heads, preferred_element_type=jnp.float32)
    weights = (within * gram).astype(jnp.bfloat16)
    grad_c = jnp.einsum("hts,sn->tn", weights, b_in, preferred_element_type=jnp.float32)
    grad_c = grad_c + jnp.einsum(
        "th,thp,hnp->tn", from_start, upstream_float, state_in, precision=lax.Precision.HIGHEST
    )
    grad_b = jnp.einsum("hts,tn->sn", weights, c_in, preferred_element_type=jnp.float32)
    grad_b = grad_b + jnp.einsum(
        "th,thp,hnp->tn", to_end, values_float, adjoint_in, precision=lax.Precision.HIGHEST
    )
    grad_b, grad_c = lax.psum((grad_b, grad_c), "tp")
    taken = inputs
    grad_w = lax.psum_scatter(
        lax.dot_general(
            taken, grad_values, (((0,), (0,)), ((), ())), preferred_element_type=jnp.float32
        ),
        "ctx",
        scatter_dimension=0,
        tiled=True,
    )
    return (grad_w, grad_b, grad_c)


def solution(mesh):
    return jax.shard_map(
        per_device,
        mesh=mesh,
        in_specs=(
            P("ctx", None),
            P("ctx", "tp"),
            P("ctx", None),
            P("ctx", None),
            P("ctx", "tp"),
            P("tp"),
            P("ctx", "tp"),
        ),
        out_specs=(P("ctx", "tp"), P("ctx", None), P("ctx", None)),
        check_vma=False,
    )
```

profile of v0, /device:TPU:1, one launch (start us, length us, event | category | flops | bytes accessed | tf_op | source)
XLA Modules:
  0.0 470.0 jit_solution(18002045809522812221)
XLA Ops:
  8.8 0.9 copy.30
  10.0 1.6 convolution_bitcast_fusion.4
  11.7 37.4 %all-gather.2 = f32[32,1,4]{2,1,0:T(1,128)S(1)} all-gather(f32[1,1,4]{2,1,0:T(1,128)S(1)} %get-tuple-element.318), channel_id=1, replica_groups=mesh['ctx'=32,'tp'=16] {'ctx'}, dimensions={0}, use_global_device_ids=true | all-gather | bytes 528 | tf_op jit(solution)/shard_map/all_gather | solution.py:9
  50.4 37.3 %all-gather.7.cloned.1.call-done = bf16[4096,256]{1,0:T(8,128)(2,1)} async-done(((bf16[128,256]{1,0:T(8,128)(2,1)}), bf16[4096,256]{1,0:T(8,128)(2,1)}) %all-gather.7.cloned.1.call-update) | async-done | bytes 2097168 | tf_op jit(solution)/shard_map/all_gather | solution.py:39
  87.7 2.0 convolution_convert_fusion
  91.0 70.0 %all-gather.9.cloned.1.call-done = f32[128,128,64]{1,2,0:T(8,128)} async-done(((f32[4,128,64]{1,2,0:T(8,128)}), f32[128,128,64]{1,2,0:T(8,128)}) %all-gather.9.cloned.1.call-update) | async-done | bytes 4194320 | tf_op jit(solution)/shard_map/all_gather | solution.py:9
  161.1 38.8 %while.30 = (s32[]{:T(128)}, f32[4,128,64]{2,1,0:T(8,128)S(1)}, s32[]{:T(128)}, f32[32,4]{1,0:T(8,128)S(1)}, f32[32,4,128,64]{2,3,1,0:T(8,128)}, /*index=5*/s32[]{:T(128)}, s32[]{:T(128)}, s32[]{:T(128)}, s32[]{:T(128)}) while((s32[]{:T(128)}, f32[4,128,64]{2,1,0:T(8,128)S(1)}, s32[]{:T(128)}, f32[32,4]{1,0:T(8,128)S(1)}, ...), condition=%wide.region_2.3_spmd.clone, body=%wide.region_1.2_spmd.clone.sunk | while | flops 131080 | bytes 917727 | solution.py:22
  175.6 0.9 constant_dynamic-slice_fusion.4
  184.1 0.9 constant_dynamic-slice_fusion.4
  186.6 0.9 constant_dynamic-slice_fusion.4
  190.2 0.9 constant_dynamic-slice_fusion.4
  195.1 0.9 constant_dynamic-slice_fusion.4
  201.2 2.6 convolution_bitcast_fusion
  204.7 29.8 %all-gather.11.cloned.1.call-done = f32[128,128,64]{1,2,0:T(8,128)} async-done(((f32[4,128,64]{1,2,0:T(8,128)}), f32[128,128,64]{1,2,0:T(8,128)}) %all-gather.11.cloned.1.call-update) | async-done | bytes 4194320 | tf_op jit(solution)/shard_map/all_gather | solution.py:9
  234.5 38.6 %while.31 = (s32[]{:T(128)}, f32[4,128,64]{2,1,0:T(8,128)S(1)}, s32[]{:T(128)}, f32[32,4]{1,0:T(8,128)S(1)}, f32[32,4,128,64]{2,3,1,0:T(8,128)}, /*index=5*/s32[]{:T(128)}, s32[]{:T(128)}) while((s32[]{:T(128)}, f32[4,128,64]{2,1,0:T(8,128)S(1)}, s32[]{:T(128)}, f32[32,4]{1,0:T(8,128)S(1)}, f32[32,4,128,64]{2,3,1,0:T(8,128)}, ...), condition=%wide.region_7.8_spmd.clone, body=%wide.region_6.7_spmd.clone.sunk | while | flops 131076 | bytes 917665 | solution.py:22
  248.9 0.9 constant_dynamic-slice_fusion.5
  253.8 0.9 constant_dynamic-slice_fusion.5
  258.6 0.9 constant_dynamic-slice_fusion.5
  264.6 0.9 constant_dynamic-slice_fusion.5
  274.5 69.8 %reduce-scatter.2.cloned.1.call-done = f32[128,256]{0,1:T(8,128)} async-done(((f32[4096,256]{0,1:T(8,128)}), f32[128,256]{0,1:T(8,128)}) %reduce-scatter.2.cloned.1.call-update) | async-done | bytes 131088 | tf_op jit(solution)/shard_map/reduce_scatter | solution.py:94
  344.3 1.7 copy.43
  346.0 114.5 %all-reduce.3.cloned.1.call-done = (f32[128,128]{1,0:T(8,128)}, f32[128,128]{1,0:T(8,128)}) async-done(((f32[128,128]{1,0:T(8,128)}, f32[128,128]{1,0:T(8,128)}), (f32[128,128]{1,0:T(8,128)}, f32[128,128]{1,0:T(8,128)})) %all-reduce.3.cloned.1.call-update) | async-done | bytes 131088 | tf_op jit(solution)/shard_map/psum | solution.py:92
  460.5 1.5 copy.68
  462.0 1.5 copy.69
  (287 shorter events, 73.9 us)
Async XLA Ops:
  7.2 80.5 %copy-start = (bf16[128,4096]{1,0:T(8,128)(2,1)S(1)}, bf16[128,4096]{1,0:T(8,128)(2,1)}, u32[]{:S(2)}) copy-start(bf16[128,4096]{1,0:T(8,128)(2,1)} %param.11) | copy-start | bytes 3145732
  7.2 82.9 %copy-start.1 = (bf16[128,128]{1,0:T(8,128)(2,1)S(1)}, bf16[128,128]{1,0:T(8,128)(2,1)}, u32[]{:S(2)}) copy-start(bf16[128,128]{1,0:T(8,128)(2,1)} %param.13) | copy-start | bytes 98308
  7.2 80.5 %all-gather.7.cloned.1.call-start = ((), (), s32[]{:S(2)}) async-start(), calls=%async_computation.2 | async-start | bytes 2162688 | tf_op jit(solution)/shard_map/all_gather | solution.py:39
  7.9 153.2 %all-gather.9.cloned.1.call-start = ((), (), s32[]{:S(2)}) async-start(), calls=%async_computation.3 | async-start | bytes 4325376 | tf_op jit(solution)/shard_map/all_gather | solution.py:9
  11.7 222.8 %all-gather.11.cloned.1.call-start = ((), (), s32[]{:S(2)}) async-start(), calls=%async_computation.4 | async-start | bytes 4325376 | tf_op jit(solution)/shard_map/all_gather | solution.py:9
  91.0 109.9 %copy-start.3 = (f32[4]{0:T(128)S(1)}, f32[4]{0:T(128)}, u32[]{:S(2)}) copy-start(f32[4]{0:T(128)} %param.16) | copy-start | bytes 52
  91.0 253.3 %reduce-scatter.2.cloned.1.call-start = ((), (), s32[]{:S(2)}) async-start(), calls=%async_computation.1 | async-start | bytes 4325376 | tf_op jit(solution)/shard_map/reduce_scatter | solution.py:94
  201.2 2.7 copy-start.2
  203.9 256.6 %all-reduce.3.cloned.1.call-start = ((), (), s32[]{:S(2)}) async-start(), calls=%async_computation.5 | async-start | bytes 262144 | tf_op jit(solution)/shard_map/psum | solution.py:92
Sparse Core Ops, SparseCore 0:
  10.1 77.5 all-gather.6
  90.4 70.6 all-gather.8
  163.2 71.1 all-gather.10
  237.1 107.1 reduce-scatter.1
  348.0 112.4 all-reduce.2
where the time goes:
time: 472 us; the launch traced here: 470 us
  waiting for transfers between devices  322 us (68%)
  local copies, waits for them, and re-layouts  74.7 us (16%)
  blocking collectives  37.4 us (8%)
  between operations  13.9 us (3%)
  matrix products  11.8 us (2%)
  other arithmetic  6.71 us (1%)
    psum x1, waiting for transfers between devices, per_device(): grad_b, grad_c = lax.psum((grad_b, grad_c), 'tp')  115 us
    all_gather x2, waiting for transfers between devices, carried_in(): everything = jax.tree.map(lambda part: lax.all_gather(part, axis), shard)  99.8 us
    reduce_scatter x1, waiting for transfers between devices, per_device(): lax.psum_scatter(lax.dot_general(taken, grad_values, (((0,), (0,)), ((),...  69.8 us
    dynamic_slice x128, local copies, waits for them, and re-layouts, step(): new = combine(before, jax.tree.map(lambda part: part[at], everything))  67 us
    all_gather x1, blocking collectives, carried_in(): everything = jax.tree.map(lambda part: lax.all_gather(part, axis), shard)  37.4 us
    all_gather x1, waiting for transfers between devices, per_device(): lax.all_gather(w_in, 'ctx', axis=0, tiled=True)  37.3 us
  transfers between devices with their start and end apart: 5, of which 5 were waited for; matrix products, arithmetic and copies ran while one was open for 19% of the time, Pallas kernels for 0%

commit v1 on v0

v1 whole, which is shorter than its diff:
```python
import functools

import jax
import jax.numpy as jnp
from jax import lax
from jax.experimental import pallas as pl
from jax.experimental.pallas import tpu as pltpu
from jax.sharding import PartitionSpec as P

F32 = jnp.float32
BF16 = jnp.bfloat16
MESH = pl.DeviceIdType.MESH
HIGHEST = lax.Precision.HIGHEST
LANES = 128
PLAIN = ((1,), (0,))
SECOND_T = ((1,), (1,))


def dot(a, b, dims=PLAIN, precision=None):
    return lax.dot_general(a, b, (dims, ((), ())), precision=precision, preferred_element_type=F32)


def split(x):
    high = x.astype(BF16)
    return high, (x - high.astype(F32)).astype(BF16)


def dot_split(a, b_pair):
    return dot(a, b_pair[0]) + dot(a, b_pair[1])


def wait_bytes(ref, sem):
    pltpu.make_async_copy(ref, ref, sem).wait()


class Ring:
    def __init__(self, chips, z, core, blocks, ring_send, sib_send, ring_recv, sib_recv):
        self.chips, self.z, self.core, self.blocks = chips, z, core, blocks
        self.ring_send, self.sib_send = ring_send, sib_send
        self.ring_recv, self.sib_recv = ring_recv, sib_recv
        self.half = chips // 2
        up, down = lax.rem(z + 1, chips), lax.rem(z + chips - 1, chips)
        self.up, self.down = 2 * up, 2 * down + 1
        self.next = jnp.where(core == 0, self.up, self.down)
        self.sibling = 2 * z + 1 - core
        self.mine = 2 * z + core

    def copy(self, block, to, send, recv):
        return pltpu.make_async_remote_copy(
            src_ref=self.blocks.at[block],
            dst_ref=self.blocks.at[block],
            send_sem=send,
            recv_sem=recv,
            device_id={"ctx": to},
            device_id_type=MESH,
        )

    def begin(self):
        self.copy(self.mine, self.up, self.ring_send, self.ring_recv.at[1, self.core]).start()
        self.copy(self.mine, self.down, self.ring_send, self.ring_recv.at[1, self.core]).start()
        self.copy(self.mine, self.sibling, self.sib_send, self.sib_recv.at[0, 0]).start()

    def source(self, k):
        back = lax.rem(self.z - k + self.chips, self.chips)
        ahead = lax.rem(self.z + k, self.chips)
        return jnp.where(self.core == 0, back, ahead)

    def sibling_source(self, k):
        back = lax.rem(self.z - k + self.chips, self.chips)
        ahead = lax.rem(self.z + k, self.chips)
        return jnp.where(self.core == 0, ahead, back)

    def step(self, k):
        if k > self.half:
            return
        base = 2 * self.source(k)
        if k == self.half:
            block = base + self.core
            wait_bytes(self.blocks.at[block], self.ring_recv.at[k, 0])
            self.copy(block, self.sibling, self.sib_send, self.sib_recv.at[k, 0]).start()
            return
        for h in range(2):
            wait_bytes(self.blocks.at[base + h], self.ring_recv.at[k, h])
            if k + 1 < self.half:
                self.copy(base + h, self.next, self.ring_send, self.ring_recv.at[k + 1, h]).start()
            self.copy(base + h, self.sibling, self.sib_send, self.sib_recv.at[k, h]).start()
        if k + 1 == self.half:
            self.copy(base + self.core, self.next, self.ring_send, self.ring_recv.at[k + 1, 0]).start()

    def arrived(self, k):
        if k == 0 or k == self.half:
            wait_bytes(self.blocks.at[0], self.sib_recv.at[k, 0])
        else:
            for h in range(2):
                wait_bytes(self.blocks.at[h], self.sib_recv.at[k, h])

    def finish(self):
        wait_bytes(self.blocks.at[pl.ds(0, self.chips - 1)], self.ring_send)
        wait_bytes(self.blocks.at[pl.ds(0, self.chips)], self.sib_send)


class Carry:
    def __init__(self, chips, z, core, worker, start, everything, found, into, sems):
        self.chips, self.z, self.core, self.worker = chips, z, core, worker
        self.start, self.everything, self.found, self.into = start, everything, found, into
        self.send1, self.recv1, self.send2, self.recv2 = [sems.at[i] for i in range(4)]
        self.mine = 2 * z + core

    def put(self, state, decay):
        slices, rows = self.chips, self.start.shape[1] - 8
        for half in range(2):
            part = state[:, half * LANES : (half + 1) * LANES]
            self.start[pl.ds(half * slices // 2, slices // 2), pl.ds(0, rows), :] = part.reshape(
                slices // 2, rows, LANES
            )
            wide = jnp.broadcast_to(decay[:, half * LANES : (half + 1) * LANES], (8, LANES))
            self.start[pl.ds(half * slices // 2, slices // 2), pl.ds(rows, 8), :] = jnp.broadcast_to(
                wide[None], (slices // 2, 8, LANES)
            )

    def send(self):
        def to(k, carry):
            chip = lax.rem(self.z + k, self.chips)
            pltpu.make_async_remote_copy(
                src_ref=self.start.at[chip],
                dst_ref=self.everything.at[self.mine],
                send_sem=self.send1,
                recv_sem=self.recv1,
                device_id={"ctx": 2 * chip + self.worker},
                device_id_type=MESH,
            ).start()
            return carry

        lax.fori_loop(1, self.chips, to, 0)

        @pl.when(self.core == self.worker)
        def _():
            pltpu.make_async_copy(
                self.start.at[self.z], self.everything.at[self.mine], self.recv1
            ).start()

        @pl.when(self.core != self.worker)
        def _():
            pltpu.make_async_remote_copy(
                src_ref=self.start.at[self.z],
                dst_ref=self.everything.at[self.mine],
                send_sem=self.send1,
                recv_sem=self.recv1,
                device_id={"ctx": 2 * self.z + self.worker},
                device_id_type=MESH,
            ).start()

    def work(self, reverse):
        count, rows = 2 * self.chips, self.start.shape[1] - 8

        @pl.when(self.core == self.worker)
        def _():
            wait_bytes(self.everything, self.recv1)

            def step(k, before):
                at = count - 1 - k if reverse else k
                self.found[at] = before.astype(BF16)
                decay = self.everything[at, pl.ds(rows, 8), :]
                state = self.everything[at, pl.ds(0, rows), :]
                wide = jnp.broadcast_to(decay[0:1, :], (rows, LANES))
                return wide * before + state

            lax.fori_loop(0, count, step, jnp.zeros((rows, LANES), F32))

            def to(k, carry):
                there = lax.rem(self.mine + k, count)
                pltpu.make_async_remote_copy(
                    src_ref=self.found.at[there],
                    dst_ref=self.into.at[self.z],
                    send_sem=self.send2,
                    recv_sem=self.recv2,
                    device_id={"ctx": there},
                    device_id_type=MESH,
                ).start()
                return carry

            lax.fori_loop(1, count, to, 0)
            pltpu.make_async_copy(
                self.found.at[self.mine], self.into.at[self.z], self.recv2
            ).start()

    def result(self):
        wait_bytes(self.into, self.recv2)
        slices = self.chips
        halves = [
            self.into[pl.ds(half * slices // 2, slices // 2)].reshape(LANES, LANES) for half in range(2)
        ]
        return jnp.concatenate(halves, axis=1)

    def finish(self):
        @pl.when(self.core == self.worker)
        def _():
            wait_bytes(self.start.at[pl.ds(0, self.chips - 1)], self.send1)
            wait_bytes(self.found.at[pl.ds(0, 2 * self.chips - 1)], self.send2)

        @pl.when(self.core != self.worker)
        def _():
            wait_bytes(self.start, self.send1)


class Total:
    def __init__(self, peers, tp, part, taken, share, full, sems):
        self.peers, self.tp = peers, tp
        self.part, self.taken, self.share, self.full = part, taken, share, full
        self.send1, self.recv1, self.send2, self.recv2 = [sems.at[i] for i in range(4)]

    def send(self, value):
        self.part[...] = value.reshape(self.part.shape)

        def to(k, carry):
            there = lax.rem(self.tp + k, self.peers)
            pltpu.make_async_remote_copy(
                src_ref=self.part.at[there],
                dst_ref=self.taken.at[self.tp],
                send_sem=self.send1,
                recv_sem=self.recv1,
                device_id={"tp": there},
                device_id_type=MESH,
            ).start()
            return carry

        lax.fori_loop(1, self.peers, to, 0)
        pltpu.make_async_copy(self.part.at[self.tp], self.taken.at[self.tp], self.recv1).start()

    def add(self):
        wait_bytes(self.taken, self.recv1)
        total = self.taken[0]
        for k in range(1, self.peers):
            total = total + self.taken[k]
        self.share[...] = total

        def to(k, carry):
            there = lax.rem(self.tp + k, self.peers)
            pltpu.make_async_remote_copy(
                src_ref=self.share,
                dst_ref=self.full.at[self.tp],
                send_sem=self.send2,
                recv_sem=self.recv2,
                device_id={"tp": there},
                device_id_type=MESH,
            ).start()
            return carry

        lax.fori_loop(1, self.peers, to, 0)
        pltpu.make_async_copy(self.share, self.full.at[self.tp], self.recv2).start()

    def result(self):
        wait_bytes(self.full, self.recv2)
        return self.full[...].reshape(LANES, LANES)

    def finish(self):
        wait_bytes(self.part.at[pl.ds(0, self.peers - 1)], self.send1)
        wait_bytes(self.full.at[pl.ds(0, self.peers - 1)], self.send2)


def kernel(
    chips, peers,
    inputs, w, b_ref, c_ref, ld_ref, skip, dout_ref,
    dw_ref, db_ref, dc_ref,
    gw, gg, cols,
    a_start, a_all, a_found, a_into,
    s_start, s_all, s_found, s_into,
    b_part, b_taken, b_share, b_full,
    c_part, c_taken, c_share, c_full,
    ring_send, ring_recv, sib_recv, carry_sems, total_sems, cols_sems,
):
    ctx, tp = lax.axis_index("ctx"), lax.axis_index("tp")
    devices = 2 * chips
    z, core = lax.div(ctx, 2), lax.rem(ctx, 2)
    heads = 4

    barrier = pltpu.get_barrier_semaphore()

    def greet_ctx(k, carry):
        pl.semaphore_signal(
            barrier, inc=1, device_id={"ctx": lax.rem(ctx + k, devices)}, device_id_type=MESH
        )
        return carry

    def greet_tp(k, carry):
        pl.semaphore_signal(
            barrier, inc=1, device_id={"tp": lax.rem(tp + k, peers)}, device_id_type=MESH
        )
        return carry

    lax.fori_loop(1, devices, greet_ctx, 0)
    lax.fori_loop(1, peers, greet_tp, 0)

    ring_w = Ring(chips, z, core, gw, ring_send.at[0], ring_send.at[1], ring_recv.at[0], sib_recv.at[0])
    ring_g = Ring(chips, z, core, gg, ring_send.at[2], ring_send.at[3], ring_recv.at[1], sib_recv.at[1])
    adjoint = Carry(chips, z, core, 0, a_start, a_all, a_found, a_into, carry_sems.at[0])
    state = Carry(chips, z, core, 1, s_start, s_all, s_found, s_into, carry_sems.at[1])
    total_b = Total(peers, tp, b_part, b_taken, b_share, b_full, total_sems.at[0])
    total_c = Total(peers, tp, c_part, c_taken, c_share, c_full, total_sems.at[1])

    gw[ctx] = w[...]
    rows = lax.broadcasted_iota(jnp.int32, (LANES, LANES), 0)
    lanes = lax.broadcasted_iota(jnp.int32, (LANES, LANES), 1)
    lower = (rows >= lanes).astype(F32)
    first = lanes < LANES // 2
    decay_log = ld_ref[...]
    wide_log = jnp.concatenate(
        [
            jnp.where(first, decay_log[:, 2 * q : 2 * q + 1], decay_log[:, 2 * q + 1 : 2 * q + 2])
            for q in range(2)
        ],
        axis=1,
    )
    cumulative = dot(lower, wide_log, precision=HIGHEST)
    block_log = cumulative[LANES - 1 : LANES, :]
    block_decay = jnp.exp(block_log)
    to_end = jnp.exp(block_log - cumulative)
    from_start = jnp.exp(cumulative)
    b, c, dout = b_ref[...], c_ref[...], dout_ref[...]
    b_t = b.astype(F32).T.astype(BF16)
    c_t = c.astype(F32).T.astype(BF16)
    dout_wide = dout.astype(F32)
    started = split(from_start * dout_wide)
    adjoint.put(dot_split(c_t, started), block_decay)

    pl.semaphore_wait(barrier, devices - 1 + peers - 1)

    ring_w.begin()
    adjoint.send()
    ring_w.step(1)

    share = 2 * LANES // peers
    cols_send1, cols_recv1, cols_send2, cols_recv2 = [cols_sems.at[i] for i in range(4)]
    cols_core = lax.div(tp * share, LANES)
    cols_row = pl.multiple_of(lax.rem(tp * share, LANES), share)

    def cols_at(device):
        return inputs.at[pl.ds(cols_row, share), pl.ds(pl.multiple_of(device * LANES, LANES), LANES)]

    @pl.when(core == cols_core)
    def _():
        def to(k, carry):
            there = lax.rem(ctx + k, devices)
            pltpu.make_async_remote_copy(
                src_ref=cols_at(there),
                dst_ref=cols.at[z, tp],
                send_sem=cols_send1,
                recv_sem=cols_recv1,
                device_id={"ctx": there},
                device_id_type=MESH,
            ).start()
            return carry

        lax.fori_loop(1, devices, to, 0)
        pltpu.make_async_copy(cols_at(ctx), cols.at[z, tp], cols_recv1).start()

    ring_w.step(2)
    adjoint.work(True)
    ring_w.step(3)

    def project(total, chip):
        at = pl.multiple_of(chip * 2 * LANES, 2 * LANES)
        block = gw[pl.ds(2 * chip, 2)].reshape(2 * LANES, -1)
        return total + dot(inputs[:, pl.ds(at, 2 * LANES)], block)

    projected = jnp.zeros((LANES, 2 * LANES), F32)
    for k in (1, 2):
        projected = project(projected, ring_w.source(k))

    scores_t = dot(b, c, SECOND_T)
    later = lanes >= rows
    within, within_t = [], []
    for h in range(heads):
        q, side = h // 2, (h % 2) * (LANES // 2)
        wide = cumulative[:, q * LANES : (q + 1) * LANES]
        column = wide[:, side : side + 1]
        row = wide.T[side : side + 1, :]
        within.append(jnp.where(rows >= lanes, jnp.exp(jnp.where(rows >= lanes, column - row, 0.0)), 0.0))
        within_t.append(jnp.where(later, jnp.exp(jnp.where(later, row - column, 0.0)), 0.0))
    local = []
    for q in range(2):
        pair = dout[:, q * LANES : (q + 1) * LANES]
        sides = [dot((within_t[2 * q + i] * scores_t).astype(BF16), pair) for i in range(2)]
        scale = jnp.where(first, skip[2 * q], skip[2 * q + 1])
        local.append(jnp.where(first, sides[0], sides[1]) + scale * pair.astype(F32))
    local = jnp.concatenate(local, axis=1)

    ring_w.step(4)
    adjoint_in = adjoint.result()
    grad_values = local + to_end * dot(b, adjoint_in)
    gg[ctx] = grad_values.astype(BF16)
    ring_g.begin()
    ring_w.step(5)

    wait_bytes(cols.at[:, tp], cols_recv1)

    def cols_to(k, carry):
        there = lax.rem(tp + k, peers)
        pltpu.make_async_remote_copy(
            src_ref=cols.at[:, tp],
            dst_ref=cols.at[:, tp],
            send_sem=cols_send2,
            recv_sem=cols_recv2,
            device_id={"tp": there},
            device_id_type=MESH,
        ).start()
        return carry

    lax.fori_loop(1, peers, cols_to, 0)

    ring_g.step(1)
    for k in range(6, chips // 2 + 1):
        ring_w.step(k)
    ring_g.step(2)

    ring_w.arrived(0)
    projected = project(projected, z)
    for k in range(1, chips // 2):
        ring_w.arrived(k)
        projected = project(projected, ring_w.sibling_source(k))
        if k > 2:
            projected = project(projected, ring_w.source(k))
    ring_w.arrived(chips // 2)
    projected = project(projected, ring_w.source(chips // 2))
    values = projected.astype(BF16)
    ended = split(to_end * values.astype(F32))
    state.put(dot_split(b_t, ended), block_decay)
    state.send()
    ring_g.step(3)

    d_b = dot(ended[0], adjoint_in, SECOND_T) + dot(ended[1], adjoint_in, SECOND_T)
    d_c = jnp.zeros((LANES, LANES), F32)
    for h in range(heads):
        q = h // 2
        mine = first if h % 2 == 0 else jnp.logical_not(first)
        part = values[:, q * LANES : (q + 1) * LANES]
        part = jnp.where(mine, part.astype(F32), 0.0).astype(BF16)
        pair = dout[:, q * LANES : (q + 1) * LANES]
        weights = (within[h] * dot(pair, part, SECOND_T)).astype(BF16)
        weights_t = (within_t[h] * dot(part, pair, SECOND_T)).astype(BF16)
        d_c = d_c + dot(weights, b)
        d_b = d_b + dot(weights_t, c)
    total_b.send(d_b)
    state.work(False)
    ring_g.step(4)
    total_b.add()
    ring_g.step(5)
    state_in = state.result()
    d_c = d_c + dot(started[0], state_in, SECOND_T) + dot(started[1], state_in, SECOND_T)
    total_c.send(d_c)
    for k in range(6, chips // 2):
        ring_g.step(k)
    total_c.add()
    for k in range(max(6, chips // 2), chips // 2 + 1):
        ring_g.step(k)

    wait_bytes(cols.at[:, pl.ds(0, peers - 1)], cols_recv2)

    def project_back(total, chip):
        return total + dot(
            cols[chip].reshape(2 * LANES, LANES).astype(F32).T.astype(BF16),
            gg[pl.ds(2 * chip, 2)].reshape(2 * LANES, -1),
        )

    ring_g.arrived(0)
    grad_w = project_back(jnp.zeros((LANES, 2 * LANES), F32), z)
    for k in range(1, chips // 2):
        grad_w = project_back(grad_w, ring_g.source(k))
        ring_g.arrived(k)
        grad_w = project_back(grad_w, ring_g.sibling_source(k))
    ring_g.arrived(chips // 2)
    dw_ref[...] = project_back(grad_w, ring_g.source(chips // 2))
    db_ref[...] = total_b.result()
    dc_ref[...] = total_c.result()

    ring_w.finish()
    ring_g.finish()
    adjoint.finish()
    state.finish()
    total_b.finish()
    total_c.finish()

    @pl.when(core == cols_core)
    def _():
        wait_bytes(inputs.at[pl.ds(0, share), pl.ds(0, (devices - 1) * LANES)], cols_send1)

    wait_bytes(cols.at[:, pl.ds(0, peers - 1)], cols_send2)


def solution(mesh):
    devices, peers = mesh.shape["ctx"], mesh.shape["tp"]
    chips = devices // 2

    def per_device(inputs, w_in, b_in, c_in, log_decay, skip, d_out):
        tokens, width = d_out.shape
        rows = LANES // (chips // 2)
        vmem = pl.BlockSpec(memory_space=pltpu.VMEM)
        carry_scratch = [
            pltpu.VMEM((chips, rows + 8, LANES), F32),
            pltpu.VMEM((devices, rows + 8, LANES), F32),
            pltpu.VMEM((devices, rows, LANES), BF16),
            pltpu.VMEM((chips, rows, LANES), BF16),
        ]
        total_scratch = [
            pltpu.VMEM((peers, tokens // peers, LANES), F32),
            pltpu.VMEM((peers, tokens // peers, LANES), F32),
            pltpu.VMEM((tokens // peers, LANES), F32),
            pltpu.VMEM((peers, tokens // peers, LANES), F32),
        ]
        half = chips // 2
        return pl.pallas_call(
            functools.partial(kernel, chips, peers),
            out_shape=(
                jax.ShapeDtypeStruct(w_in.shape, F32),
                jax.ShapeDtypeStruct(b_in.shape, F32),
                jax.ShapeDtypeStruct(c_in.shape, F32),
            ),
            in_specs=[vmem] * 5 + [pl.BlockSpec(memory_space=pltpu.SMEM), vmem],
            out_specs=(vmem, vmem, vmem),
            scratch_shapes=[
                pltpu.VMEM((devices, tokens, width), BF16),
                pltpu.VMEM((devices, tokens, width), BF16),
                pltpu.VMEM((chips, peers, 2 * tokens // peers, LANES), BF16),
            ]
            + carry_scratch * 2
            + total_scratch * 2
            + [
                pltpu.SemaphoreType.DMA((4,)),
                pltpu.SemaphoreType.DMA((2, half + 1, 2)),
                pltpu.SemaphoreType.DMA((2, half + 1, 2)),
                pltpu.SemaphoreType.DMA((2, 4)),
                pltpu.SemaphoreType.DMA((2, 4)),
                pltpu.SemaphoreType.DMA((4,)),
            ],
            compiler_params=pltpu.CompilerParams(
                collective_id=0, has_side_effects=True, vmem_limit_bytes=48 * 1024 * 1024
            ),
        )(inputs, w_in, b_in, c_in, log_decay, skip, d_out)

    return jax.shard_map(
        per_device,
        mesh=mesh,
        in_specs=(
            P("ctx", None),
            P("ctx", "tp"),
            P("ctx", None),
            P("ctx", None),
            P("ctx", "tp"),
            P("tp"),
            P("ctx", "tp"),
        ),
        out_specs=(P("ctx", "tp"), P("ctx", None), P("ctx", None)),
        check_vma=False,
    )
```

time: 472 us -> 97.9 us (0.21)
  waiting for transfers between devices: 322 us -> 0 us
  Pallas kernels: 0 us -> 90.5 us
  local copies, waits for them, and re-layouts: 74.7 us -> 6.33 us
  blocking collectives: 37.4 us -> 0 us
  between operations: 13.9 us -> 0.67 us
  matrix products: 11.8 us -> 0 us
  other arithmetic: 6.71 us -> 0 us
    all_gather x3 -> x0, waiting for transfers between devices: 137 us -> none  [the longest x2 99.8 us: carried_in(): everything = jax.tree.map(lambda part: lax.all_gather(part, axis), shard)]
    psum x1 -> x0, waiting for transfers between devices: 115 us -> none  [per_device(): grad_b, grad_c = lax.psum((grad_b, grad_c), 'tp')]
    pallas_call x0 -> x1, Pallas kernels: none -> 90.5 us  [per_device(): pl.pallas_call(functools.partial(kernel, chips, peers), out_shape=(jax.Sh...]
    reduce_scatter x1 -> x0, waiting for transfers between devices: 69.8 us -> none  [per_device(): lax.psum_scatter(lax.dot_general(taken, grad_values, (((0,), (0,)), ((),...]
    dynamic_slice x128 -> x0, local copies, waits for them, and re-layouts: 67 us -> none  [step(): new = combine(before, jax.tree.map(lambda part: part[at], everything))]
    all_gather x1 -> x0, blocking collectives: 37.4 us -> none  [carried_in(): everything = jax.tree.map(lambda part: lax.all_gather(part, axis), shard)]
    dot_general x12 -> x0, matrix products: 11.8 us -> none  [the longest x1 2.64 us: per_device(): lax.dot_general(taken, grad_values, (((0,), (0,)), ((), ())), preferred_e...]
    select_n x64 -> x0, other arithmetic: 6.47 us -> none  [step(): return jax.tree.map(lambda a, b: jnp.where(reached, a, b), new, before)]
  transfers between devices with their start and end apart: 5 -> 0, of which waited for: 5 -> 0; matrix products, arithmetic and copies ran while one was open for 19% -> 0% of each run, Pallas kernels for 0% -> 0%
where the time goes in v1:
time: 97.9 us; the launch traced here: 97.5 us
  Pallas kernels  90.5 us (92%)
  local copies, waits for them, and re-layouts  6.33 us (6%)
    pallas_call x1, Pallas kernels, per_device(): pl.pallas_call(functools.partial(kernel, chips, peers), out_shape=(jax.Sh...  90.5 us
    unnamed x16, local copies, waits for them, and re-layouts  6.33 us

profile of v1, /device:TPU:1, one launch (start us, length us, event | category | flops | bytes accessed | tf_op | source)
XLA Modules:
  0.0 97.5 jit_solution(4960650755519803567)
XLA Ops:
  0.6 0.0 copy-start.5
  0.6 0.0 copy-start.1
  0.7 0.8 copy.10.ld_ref
  1.5 0.0 copy-done.5
  1.5 0.0 copy-done.1
  1.5 0.0 copy-start
  1.5 1.2 %copy-done = bf16[128,4096]{1,0:T(8,128)(2,1)S(1)} copy-done((bf16[128,4096]{1,0:T(8,128)(2,1)S(1)}, bf16[128,4096]{1,0:T(8,128)(2,1)}, u32[]{:S(2)}) %copy-start) | copy-done | bytes 1048600
  2.7 0.0 copy-start.2
  2.7 0.8 copy-done.2
  3.6 0.0 copy-start.3
  3.6 0.8 copy-done.3
  4.3 0.0 copy-start.4
  4.3 0.8 copy-done.4
  5.1 90.5 %shard_map.94 = (f32[128,256]{1,0:T(8,128)S(1)}, f32[128,128]{1,0:T(8,128)S(1)}, f32[128,128]{1,0:T(8,128)S(1)}) custom-call(bf16[128,4096]{1,0:T(8,128)(2,1)S(1)} %copy-done, bf16[128,256]{1,0:T(8,128)(2,1)S(1)} %copy-done.1, bf16[128,128]{1,0:T(8,128)(2,1)S(1)} %copy-done.3, bf16[128,128]{1,0:T(8,128)(2,1)S(1)} %copy-done.4, f32[128,4]{1,0:T(8,128)S(1)} %copy.10.ld_ref, ...), custom_call_target="tpu_custom_call" | custom-call | tf_op jit(solution)/shard_map/pallas_call | solution.py:511
  95.6 0.7 copy.14
  96.2 0.6 copy.15
  96.8 0.6 copy.16
Async XLA Ops:
  0.6 0.8 copy-start.5
  0.6 0.8 copy-start.1
  1.5 1.2 %copy-start = (bf16[128,4096]{1,0:T(8,128)(2,1)S(1)}, bf16[128,4096]{1,0:T(8,128)(2,1)}, u32[]{:S(2)}) copy-start(bf16[128,4096]{1,0:T(8,128)(2,1)} %inputs.1) | copy-start | bytes 3145732
  2.7 0.8 copy-start.2
  3.6 0.8 copy-start.3
  4.3 0.8 copy-start.4

commit v2 on v1

v2 whole, which is shorter than its diff:
```python
import functools

import jax
import jax.numpy as jnp
from jax import lax
from jax.experimental import pallas as pl
from jax.experimental.pallas import tpu as pltpu
from jax.sharding import PartitionSpec as P

F32 = jnp.float32
BF16 = jnp.bfloat16
MESH = pl.DeviceIdType.MESH
HIGHEST = lax.Precision.HIGHEST
LANES = 128
PLAIN = ((1,), (0,))
SECOND_T = ((1,), (1,))


def dot(a, b, dims=PLAIN, precision=None):
    return lax.dot_general(a, b, (dims, ((), ())), precision=precision, preferred_element_type=F32)


def split(x):
    high = x.astype(BF16)
    return high, (x - high.astype(F32)).astype(BF16)


def dot_split(a, b_pair):
    return dot(a, b_pair[0]) + dot(a, b_pair[1])


def carried(a_pair, b_pair):
    return sum(dot(a_pair[i], b_pair[j], SECOND_T) for i, j in ((0, 0), (0, 1), (1, 0)))


def wait_bytes(ref, sem):
    pltpu.make_async_copy(ref, ref, sem).wait()


def far_first(place, i, count):
    aside = lax.div(i + 1, 2)
    return lax.rem(place + count // 2 + jnp.where(lax.rem(i, 2) == 1, count - aside, aside), count)


class Ring:
    def __init__(self, chips, stride, z, core, blocks, ring_send, sib_send, ring_recv, sib_recv):
        self.chips, self.stride, self.half = chips, stride, chips // 2
        self.z, self.core, self.blocks = z, core, blocks
        self.ring_send, self.sib_send = ring_send, sib_send
        self.ring_recv, self.sib_recv = ring_recv, sib_recv
        self.sibling, self.mine = 2 * z + 1 - core, 2 * z + core

    def copy(self, block, to, send, recv):
        pltpu.make_async_remote_copy(
            src_ref=self.blocks.at[block],
            dst_ref=self.blocks.at[block],
            send_sem=send,
            recv_sem=recv,
            device_id={"ctx": to},
            device_id_type=MESH,
        ).start()

    def back(self, k):
        return lax.rem(self.z + (self.chips - k), self.chips)

    def ahead(self, k):
        return lax.rem(self.z + k, self.chips)

    def source(self, k):
        return jnp.where(self.core == 0, self.back(k), self.ahead(k))

    def sibling_source(self, k):
        return jnp.where(self.core == 0, self.ahead(k), self.back(k))

    def begin(self):
        for s in range(self.stride, 0, -1):
            recv = self.ring_recv.at[s, self.core]
            self.copy(self.mine, 2 * self.ahead(s), self.ring_send, recv)
            self.copy(self.mine, 2 * self.back(s) + 1, self.ring_send, recv)
        self.copy(self.mine, self.sibling, self.sib_send, self.sib_recv.at[0, 0])

    def step(self, k):
        if k > self.half:
            return
        base = 2 * self.source(k)
        if k == self.half:
            block = base + self.core
            wait_bytes(self.blocks.at[block], self.ring_recv.at[k, 0])
            self.copy(block, self.sibling, self.sib_send, self.sib_recv.at[k, 0])
            return
        onward = [s for s in range(self.stride, 0, -1) if k % self.stride == 0 and k + s <= self.half]
        for h in range(2):
            wait_bytes(self.blocks.at[base + h], self.ring_recv.at[k, h])
            for s in onward:
                if k + s < self.half:
                    to = 2 * self.sibling_source(s) + self.core
                    self.copy(base + h, to, self.ring_send, self.ring_recv.at[k + s, h])
            self.copy(base + h, self.sibling, self.sib_send, self.sib_recv.at[k, h])
        for s in onward:
            if k + s == self.half:
                to = 2 * self.sibling_source(s) + self.core
                self.copy(base + self.core, to, self.ring_send, self.ring_recv.at[k + s, 0])

    def arrived(self, k):
        if k == 0 or k == self.half:
            wait_bytes(self.blocks.at[0], self.sib_recv.at[k, 0])
        else:
            for h in range(2):
                wait_bytes(self.blocks.at[h], self.sib_recv.at[k, h])

    def finish(self):
        wait_bytes(self.blocks.at[pl.ds(0, self.chips - 1)], self.ring_send)
        wait_bytes(self.blocks.at[pl.ds(0, self.chips)], self.sib_send)


class Carry:
    def __init__(self, chips, z, core, near, decays, refs, sems):
        self.chips, self.z, self.core, self.near = chips, z, core, near
        self.start, self.peer, self.joined, self.everything, self.found, self.into = refs
        self.peer_send, self.peer_recv, self.send1, self.recv1, self.send2, self.send3, self.recv2 = [
            sems.at[i] for i in range(7)
        ]
        self.rows = self.into.shape[1]
        self.decays = self.everything if decays is None else decays
        self.sent = self.everything.shape[1]

    def put(self, state, decay):
        slices, rows = self.chips, self.rows
        for half in range(2):
            at = pl.ds(half * slices // 2, slices // 2)
            part = state[:, half * LANES : (half + 1) * LANES]
            self.start[at, pl.ds(0, rows), :] = part.reshape(slices // 2, rows, LANES)
            wide = jnp.broadcast_to(decay[:, half * LANES : (half + 1) * LANES], (8, LANES))
            self.start[at, pl.ds(rows, 8), :] = jnp.broadcast_to(wide[None], (slices // 2, 8, LANES))

    def hand(self):
        @pl.when(self.core == self.near)
        def _():
            pltpu.make_async_remote_copy(
                src_ref=self.start,
                dst_ref=self.peer,
                send_sem=self.peer_send,
                recv_sem=self.peer_recv,
                device_id={"ctx": 2 * self.z + 1 - self.near},
                device_id_type=MESH,
            ).start()
            self.peer[:, pl.ds(0, self.rows), :] = jnp.zeros((self.chips, self.rows, LANES), F32)
            self.peer[:, pl.ds(self.rows, 8), :] = jnp.ones((self.chips, 8, LANES), F32)

    def send(self):
        rows = self.rows

        @pl.when(self.core != self.near)
        def _():
            wait_bytes(self.peer, self.peer_recv)
            decay = self.start[:, rows : rows + 1, :]
            self.joined[:, pl.ds(0, rows), :] = self.start[:, 0:rows, :] + decay * self.peer[:, 0:rows, :]
            self.joined[:, pl.ds(rows, 8), :] = decay * self.peer[:, rows : rows + 8, :]

            def copy(chip):
                return dict(
                    src_ref=self.joined.at[chip, pl.ds(0, self.sent)],
                    dst_ref=self.everything.at[self.z],
                )

            def to(i, carry):
                chip = far_first(self.z, i, self.chips)
                pltpu.make_async_remote_copy(
                    **copy(chip),
                    send_sem=self.send1,
                    recv_sem=self.recv1,
                    device_id={"ctx": 2 * chip},
                    device_id_type=MESH,
                ).start()
                return carry

            lax.fori_loop(0, self.chips - 1, to, 0)
            if self.near == 1:
                pltpu.make_async_copy(*copy(self.z).values(), self.recv1).start()
            else:
                pltpu.make_async_remote_copy(
                    **copy(self.z),
                    send_sem=self.send1,
                    recv_sem=self.recv1,
                    device_id={"ctx": 2 * self.z},
                    device_id_type=MESH,
                ).start()

    def work(self):
        count, rows = self.chips, self.rows

        @pl.when(self.core == 0)
        def _():
            wait_bytes(self.everything, self.recv1)
            before = jnp.zeros((rows, LANES), F32)
            for k in range(count):
                at = count - 1 - k if self.near == 1 else k
                self.found[at] = before.astype(BF16)
                decay = jnp.broadcast_to(self.decays[at, rows : rows + 1, :], (rows, LANES))
                before = decay * before + self.everything[at, 0:rows, :]

            def copy(chip, core):
                return pltpu.make_async_remote_copy(
                    src_ref=self.found.at[chip],
                    dst_ref=self.into.at[self.z],
                    send_sem=self.send3 if core else self.send2,
                    recv_sem=self.recv2,
                    device_id={"ctx": 2 * chip + core},
                    device_id_type=MESH,
                )

            def to(i, carry):
                chip = far_first(self.z, i, count)
                copy(chip, 0).start()
                copy(chip, 1).start()
                return carry

            lax.fori_loop(0, count - 1, to, 0)
            copy(self.z, 1).start()
            pltpu.make_async_copy(self.found.at[self.z], self.into.at[self.z], self.recv2).start()

    def result(self):
        wait_bytes(self.into, self.recv2)
        halves = []
        for half in range(2):
            at = pl.ds(half * self.chips // 2, self.chips // 2)
            peer = self.peer[at]
            decay = peer[:, self.rows : self.rows + 1, :]
            part = decay * self.into[at].astype(F32) + peer[:, 0 : self.rows, :]
            halves.append(part.reshape(LANES, LANES))
        return split(jnp.concatenate(halves, axis=1))

    def finish(self):
        @pl.when(self.core == self.near)
        def _():
            wait_bytes(self.start, self.peer_send)

        @pl.when(self.core != self.near)
        def _():
            wait_bytes(self.joined.at[pl.ds(0, self.chips - self.near), pl.ds(0, self.sent)], self.send1)

        @pl.when(self.core == 0)
        def _():
            wait_bytes(self.found.at[pl.ds(0, self.chips - 1)], self.send2)
            wait_bytes(self.found, self.send3)


class Total:
    def __init__(self, peers, tp, part, taken, share, full, sems):
        self.peers, self.tp = peers, tp
        self.part, self.taken, self.share, self.full = part, taken, share, full
        self.send1, self.recv1, self.send2, self.recv2 = [sems.at[i] for i in range(4)]

    def send(self, value):
        self.part[...] = value.reshape(self.part.shape)

        def to(k, carry):
            there = lax.rem(self.tp + k, self.peers)
            pltpu.make_async_remote_copy(
                src_ref=self.part.at[there],
                dst_ref=self.taken.at[self.tp],
                send_sem=self.send1,
                recv_sem=self.recv1,
                device_id={"tp": there},
                device_id_type=MESH,
            ).start()
            return carry

        lax.fori_loop(1, self.peers, to, 0)
        pltpu.make_async_copy(self.part.at[self.tp], self.taken.at[self.tp], self.recv1).start()

    def add(self):
        wait_bytes(self.taken, self.recv1)
        total = self.taken[0]
        for k in range(1, self.peers):
            total = total + self.taken[k]
        self.share[...] = total

        def to(k, carry):
            there = lax.rem(self.tp + k, self.peers)
            pltpu.make_async_remote_copy(
                src_ref=self.share,
                dst_ref=self.full.at[self.tp],
                send_sem=self.send2,
                recv_sem=self.recv2,
                device_id={"tp": there},
                device_id_type=MESH,
            ).start()
            return carry

        lax.fori_loop(1, self.peers, to, 0)
        pltpu.make_async_copy(self.share, self.full.at[self.tp], self.recv2).start()

    def result(self):
        wait_bytes(self.full, self.recv2)
        return self.full[...].reshape(LANES, LANES)

    def finish(self):
        wait_bytes(self.part.at[pl.ds(0, self.peers - 1)], self.send1)
        wait_bytes(self.full.at[pl.ds(0, self.peers - 1)], self.send2)


class Columns:
    def __init__(self, chips, peers, ctx, z, core, tp, inputs, cols, sems):
        self.devices, self.peers = 2 * chips, peers
        self.ctx, self.z, self.core, self.tp = ctx, z, core, tp
        self.inputs, self.cols = inputs, cols
        self.send1, self.recv1, self.send2, self.recv2 = [sems.at[i] for i in range(4)]
        self.share = 2 * LANES // peers
        self.sender = lax.div(tp * self.share, LANES)
        self.row = pl.multiple_of(lax.rem(tp * self.share, LANES), self.share)

    def block(self, device):
        at = pl.multiple_of(device * LANES, LANES)
        return self.inputs.at[pl.ds(self.row, self.share), pl.ds(at, LANES)]

    def send(self):
        @pl.when(self.core == self.sender)
        def _():
            def to(k, carry):
                there = lax.rem(self.ctx + k, self.devices)
                pltpu.make_async_remote_copy(
                    src_ref=self.block(there),
                    dst_ref=self.cols.at[self.z, self.tp],
                    send_sem=self.send1,
                    recv_sem=self.recv1,
                    device_id={"ctx": there},
                    device_id_type=MESH,
                ).start()
                return carry

            lax.fori_loop(1, self.devices, to, 0)
            pltpu.make_async_copy(
                self.block(self.ctx), self.cols.at[self.z, self.tp], self.recv1
            ).start()

    def spread(self):
        mine = self.cols.at[:, self.tp]
        wait_bytes(mine, self.recv1)

        def to(k, carry):
            there = lax.rem(self.tp + k, self.peers)
            pltpu.make_async_remote_copy(
                src_ref=mine,
                dst_ref=mine,
                send_sem=self.send2,
                recv_sem=self.recv2,
                device_id={"tp": there},
                device_id_type=MESH,
            ).start()
            return carry

        lax.fori_loop(1, self.peers, to, 0)

    def arrived(self):
        wait_bytes(self.cols.at[:, pl.ds(0, self.peers - 1)], self.recv2)

    def finish(self):
        @pl.when(self.core == self.sender)
        def _():
            sent = self.inputs.at[pl.ds(0, self.share), pl.ds(0, (self.devices - 1) * LANES)]
            wait_bytes(sent, self.send1)

        wait_bytes(self.cols.at[:, pl.ds(0, self.peers - 1)], self.send2)


def kernel(
    chips, peers,
    inputs_hbm, w_hbm, b_hbm, c_hbm, ld_hbm, skip, dout_hbm,
    dw_ref, db_ref, dc_ref,
    inputs, b_ref, c_ref, ld_ref, dout_ref,
    gw, gg, cols,
    a_start, a_peer, a_joined, a_all, a_found, a_into,
    s_start, s_peer, s_joined, s_all, s_found, s_into,
    b_part, b_taken, b_share, b_full,
    c_part, c_taken, c_share, c_full,
    ring_send, ring_recv, sib_recv, carry_sems, total_sems, cols_sems, fetch_sems,
):
    ctx, tp = lax.axis_index("ctx"), lax.axis_index("tp")
    devices = 2 * chips
    z, core = lax.div(ctx, 2), lax.rem(ctx, 2)
    heads = 4

    fetches = [
        pltpu.make_async_copy(there, here, fetch_sems.at[i])
        for i, (there, here) in enumerate(
            [
                (ld_hbm, ld_ref),
                (c_hbm, c_ref),
                (dout_hbm, dout_ref),
                (b_hbm, b_ref),
                (w_hbm, gw.at[ctx]),
                (inputs_hbm, inputs),
            ]
        )
    ]
    for fetch in fetches:
        fetch.start()

    barrier = pltpu.get_barrier_semaphore()

    def greet_ctx(k, carry):
        pl.semaphore_signal(
            barrier, inc=1, device_id={"ctx": lax.rem(ctx + k, devices)}, device_id_type=MESH
        )
        return carry

    def greet_tp(k, carry):
        pl.semaphore_signal(
            barrier, inc=1, device_id={"tp": lax.rem(tp + k, peers)}, device_id_type=MESH
        )
        return carry

    lax.fori_loop(1, devices, greet_ctx, 0)
    lax.fori_loop(1, peers, greet_tp, 0)

    ring_w = Ring(
        chips, 2, z, core, gw, ring_send.at[0], ring_send.at[1], ring_recv.at[0], sib_recv.at[0]
    )
    ring_g = Ring(
        chips, 2, z, core, gg, ring_send.at[2], ring_send.at[3], ring_recv.at[1], sib_recv.at[1]
    )
    adjoint = Carry(
        chips, z, core, 1, None, (a_start, a_peer, a_joined, a_all, a_found, a_into), carry_sems.at[0]
    )
    state = Carry(
        chips, z, core, 0, a_all, (s_start, s_peer, s_joined, s_all, s_found, s_into), carry_sems.at[1]
    )
    total_b = Total(peers, tp, b_part, b_taken, b_share, b_full, total_sems.at[0])
    columns = Columns(chips, peers, ctx, z, core, tp, inputs, cols, cols_sems)
    total_c = Total(peers, tp, c_part, c_taken, c_share, c_full, total_sems.at[1])

    rows = lax.broadcasted_iota(jnp.int32, (LANES, LANES), 0)
    lanes = lax.broadcasted_iota(jnp.int32, (LANES, LANES), 1)
    upper = (rows <= lanes).astype(F32)
    first, first_rows = lanes < LANES // 2, rows < LANES // 2
    for fetch in fetches[:4]:
        fetch.wait()
    cumulative_t = []
    for q in range(2):
        pair = [jnp.broadcast_to(ld_ref[2 * q + i : 2 * q + i + 1, :], (LANES, LANES)) for i in range(2)]
        cumulative_t.append(dot(jnp.where(first_rows, pair[0], pair[1]), upper, precision=HIGHEST))
    cumulative = jnp.concatenate([part.T for part in cumulative_t], axis=1)
    block_log = cumulative[LANES - 1 : LANES, :]
    block_decay = jnp.exp(block_log)
    to_end = jnp.exp(block_log - cumulative)
    from_start = jnp.exp(cumulative)
    b, c, dout = b_ref[...], c_ref[...], dout_ref[...]
    b_t = b.astype(F32).T.astype(BF16)
    c_t = c.astype(F32).T.astype(BF16)
    dout_wide = dout.astype(F32)
    started = split(from_start * dout_wide)
    adjoint.put(dot_split(c_t, started), block_decay)

    pl.semaphore_wait(barrier, devices - 1 + peers - 1)
    for fetch in fetches[4:]:
        fetch.wait()

    ring_w.begin()
    adjoint.hand()
    adjoint.send()
    ring_w.step(2)
    ring_w.step(1)
    columns.send()

    def project(total, chip):
        at = pl.multiple_of(chip * 2 * LANES, 2 * LANES)
        block = gw[pl.ds(2 * chip, 2)].reshape(2 * LANES, -1)
        return total + dot(inputs[:, pl.ds(at, 2 * LANES)], block)

    ring_w.step(4)
    ring_w.step(3)
    ring_w.arrived(0)
    projected = project(jnp.zeros((LANES, 2 * LANES), F32), z)
    for k in (1, 2):
        projected = project(projected, ring_w.source(k))
        ring_w.arrived(k)
        projected = project(projected, ring_w.sibling_source(k))
    adjoint.work()
    ring_w.step(6)
    ring_w.step(5)

    scores_t = dot(b, c, SECOND_T)
    later = lanes >= rows
    within, within_t = [], []
    for h in range(heads):
        q, side = h // 2, (h % 2) * (LANES // 2)
        column = cumulative[:, q * LANES + side : q * LANES + side + 1]
        row = cumulative_t[q][side : side + 1, :]
        within.append(jnp.where(rows >= lanes, jnp.exp(jnp.where(rows >= lanes, column - row, 0.0)), 0.0))
        within_t.append(jnp.where(later, jnp.exp(jnp.where(later, row - column, 0.0)), 0.0))
    local = []
    for q in range(2):
        pair = dout[:, q * LANES : (q + 1) * LANES]
        sides = [dot((within_t[2 * q + i] * scores_t).astype(BF16), pair) for i in range(2)]
        scale = jnp.where(first, skip[2 * q], skip[2 * q + 1])
        local.append(jnp.where(first, sides[0], sides[1]) + scale * pair.astype(F32))
    local = jnp.concatenate(local, axis=1)

    columns.spread()
    for k in range(3, chips // 2 - 1):
        projected = project(projected, ring_w.source(k))
        ring_w.arrived(k)
        projected = project(projected, ring_w.sibling_source(k))
    ring_w.step(8)
    ring_w.step(7)

    k = chips // 2 - 1
    projected = project(projected, ring_w.source(k))
    ring_w.arrived(k)
    projected = project(projected, ring_w.sibling_source(k))
    ring_w.arrived(chips // 2)
    projected = project(projected, ring_w.source(chips // 2))
    values = projected.astype(BF16)
    ended = split(to_end * values.astype(F32))
    state.put(dot_split(b_t, ended), block_decay)
    state.hand()

    adjoint_in = adjoint.result()
    grad_values = local + to_end * dot_split(b, adjoint_in)
    gg[ctx] = grad_values.astype(BF16)
    ring_g.begin()
    state.send()

    d_b = carried(ended, adjoint_in)
    d_c = jnp.zeros((LANES, LANES), F32)
    for h in range(heads):
        q = h // 2
        mine = first if h % 2 == 0 else jnp.logical_not(first)
        part = values[:, q * LANES : (q + 1) * LANES]
        part = jnp.where(mine, part.astype(F32), 0.0).astype(BF16)
        pair = dout[:, q * LANES : (q + 1) * LANES]
        weights = (within[h] * dot(pair, part, SECOND_T)).astype(BF16)
        weights_t = (within_t[h] * dot(part, pair, SECOND_T)).astype(BF16)
        d_c = d_c + dot(weights, b)
        d_b = d_b + dot(weights_t, c)
    total_b.send(d_b)
    ring_g.step(2)
    ring_g.step(1)
    ring_g.step(4)
    ring_g.step(3)
    state.work()
    total_b.add()
    ring_g.step(6)
    ring_g.step(5)
    state_in = state.result()
    d_c = d_c + carried(started, state_in)
    total_c.send(d_c)
    ring_g.step(8)
    ring_g.step(7)
    total_c.add()

    columns.arrived()

    def project_back(total, chip):
        return total + dot(
            cols[chip].reshape(2 * LANES, LANES).astype(F32).T.astype(BF16),
            gg[pl.ds(2 * chip, 2)].reshape(2 * LANES, -1),
        )

    ring_g.arrived(0)
    grad_w = project_back(jnp.zeros((LANES, 2 * LANES), F32), z)
    for k in range(1, chips // 2):
        grad_w = project_back(grad_w, ring_g.source(k))
        ring_g.arrived(k)
        grad_w = project_back(grad_w, ring_g.sibling_source(k))
    ring_g.arrived(chips // 2)
    dw_ref[...] = project_back(grad_w, ring_g.source(chips // 2))
    db_ref[...] = total_b.result()
    dc_ref[...] = total_c.result()

    ring_w.finish()
    ring_g.finish()
    adjoint.finish()
    state.finish()
    total_b.finish()
    total_c.finish()
    columns.finish()


def solution(mesh):
    devices, peers = mesh.shape["ctx"], mesh.shape["tp"]
    chips = devices // 2

    def per_device(inputs, w_in, b_in, c_in, log_decay, skip, d_out):
        tokens, width = d_out.shape
        rows = LANES // (chips // 2)
        vmem, hbm = pl.BlockSpec(memory_space=pltpu.VMEM), pl.BlockSpec(memory_space=pltpu.HBM)
        def carry_scratch(sent):
            return [
                pltpu.VMEM((chips, rows + 8, LANES), F32),
                pltpu.VMEM((chips, rows + 8, LANES), F32),
                pltpu.VMEM((chips, rows + 8, LANES), F32),
                pltpu.VMEM((chips, sent, LANES), F32),
                pltpu.VMEM((chips, rows, LANES), BF16),
                pltpu.VMEM((chips, rows, LANES), BF16),
            ]

        total_scratch = [
            pltpu.VMEM((peers, tokens // peers, LANES), F32),
            pltpu.VMEM((peers, tokens // peers, LANES), F32),
            pltpu.VMEM((tokens // peers, LANES), F32),
            pltpu.VMEM((peers, tokens // peers, LANES), F32),
        ]
        half = chips // 2
        return pl.pallas_call(
            functools.partial(kernel, chips, peers),
            out_shape=(
                jax.ShapeDtypeStruct(w_in.shape, F32),
                jax.ShapeDtypeStruct(b_in.shape, F32),
                jax.ShapeDtypeStruct(c_in.shape, F32),
            ),
            in_specs=[hbm] * 5 + [pl.BlockSpec(memory_space=pltpu.SMEM), hbm],
            out_specs=(vmem, vmem, vmem),
            scratch_shapes=[
                pltpu.VMEM(inputs.shape, BF16),
                pltpu.VMEM(b_in.shape, BF16),
                pltpu.VMEM(c_in.shape, BF16),
                pltpu.VMEM(log_decay.shape[::-1], F32),
                pltpu.VMEM(d_out.shape, BF16),
                pltpu.VMEM((devices, tokens, width), BF16),
                pltpu.VMEM((devices, tokens, width), BF16),
                pltpu.VMEM((chips, peers, 2 * tokens // peers, LANES), BF16),
            ]
            + carry_scratch(rows + 8)
            + carry_scratch(rows)
            + total_scratch * 2
            + [
                pltpu.SemaphoreType.DMA((4,)),
                pltpu.SemaphoreType.DMA((2, half + 1, 2)),
                pltpu.SemaphoreType.DMA((2, half + 1, 2)),
                pltpu.SemaphoreType.DMA((2, 7)),
                pltpu.SemaphoreType.DMA((2, 4)),
                pltpu.SemaphoreType.DMA((4,)),
                pltpu.SemaphoreType.DMA((6,)),
            ],
            compiler_params=pltpu.CompilerParams(
                collective_id=0, has_side_effects=True, vmem_limit_bytes=60 * 1024 * 1024
            ),
        )(inputs, w_in, b_in, c_in, log_decay.T, skip, d_out)

    return jax.shard_map(
        per_device,
        mesh=mesh,
        in_specs=(
            P("ctx", None),
            P("ctx", "tp"),
            P("ctx", None),
            P("ctx", None),
            P("ctx", "tp"),
            P("tp"),
            P("ctx", "tp"),
        ),
        out_specs=(P("ctx", "tp"), P("ctx", None), P("ctx", None)),
        check_vma=False,
    )
```

time: 97.9 us -> 84.7 us (0.87)
  Pallas kernels: 90.5 us -> 80.7 us
  local copies, waits for them, and re-layouts: 6.33 us -> 3.09 us
    pallas_call x1, Pallas kernels: 90.5 us -> 80.7 us  [per_device(): pl.pallas_call(functools.partial(kernel, chips, peers), out_shape=(jax.Sh...]
    unnamed x16 -> x7, local copies, waits for them, and re-layouts: 6.33 us -> 3.09 us
where the time goes in v2:
time: 84.7 us; the launch traced here: 84.5 us
  Pallas kernels  80.7 us (95%)
  local copies, waits for them, and re-layouts  3.09 us (4%)
    pallas_call x1, Pallas kernels, per_device(): pl.pallas_call(functools.partial(kernel, chips, peers), out_shape=(jax.Sh...  80.7 us
    unnamed x7, local copies, waits for them, and re-layouts  3.09 us

profile of v2, /device:TPU:1, one launch (start us, length us, event | category | flops | bytes accessed | tf_op | source)
XLA Modules:
  0.0 84.5 jit_solution(9391656116649085028)
XLA Ops:
  0.6 80.7 %shard_map.94 = (f32[128,256]{1,0:T(8,128)}, f32[128,128]{1,0:T(8,128)}, f32[128,128]{1,0:T(8,128)}) custom-call(bf16[128,4096]{1,0:T(8,128)(2,1)} %inputs_hbm.1, bf16[128,256]{1,0:T(8,128)(2,1)} %w_hbm.1, bf16[128,128]{1,0:T(8,128)(2,1)} %b_hbm.1, bf16[128,128]{1,0:T(8,128)(2,1)} %c_hbm.1, f32[4,128]{1,0:T(4,128)} %bitcast.1, f32[4]{0:T(128)} %skip.1, ...), custom_call_target="tpu_custom_call" | custom-call | tf_op jit(solution)/shard_map/pallas_call | solution.py:606
  81.4 0.0 copy-start.1
  81.4 1.6 %copy.13 = f32[128,256]{1,0:T(8,128)} copy(f32[128,256]{1,0:T(8,128)} %get-tuple-element.6) | data formatting | bytes 262144
  83.0 0.0 copy-done.1
  83.0 0.0 copy-start
  83.0 0.6 copy.14
  83.6 0.2 copy-done
  83.8 0.6 copy.15
Async XLA Ops:
  81.4 1.6 %copy-start.1 = (f32[128,128]{1,0:T(8,128)S(1)}, f32[128,128]{1,0:T(8,128)}, u32[]{:S(2)}) copy-start(f32[128,128]{1,0:T(8,128)} %get-tuple-element.7) | copy-start | bytes 196612
  83.0 0.9 %copy-start = (f32[128,128]{1,0:T(8,128)S(1)}, f32[128,128]{1,0:T(8,128)}, u32[]{:S(2)}) copy-start(f32[128,128]{1,0:T(8,128)} %get-tuple-element.8) | copy-start | bytes 196612

commit v3 on v2

--- a/solution.py
+++ b/solution.py
@@ -117,8 +117,8 @@
     def __init__(self, chips, z, core, near, decays, refs, sems):
         self.chips, self.z, self.core, self.near = chips, z, core, near
         self.start, self.peer, self.joined, self.everything, self.found, self.into = refs
-        self.peer_send, self.peer_recv, self.send1, self.recv1, self.send2, self.send3, self.recv2 = [
-            sems.at[i] for i in range(7)
+        self.peer_send, self.peer_recv, self.send1, self.recv1, self.send2, self.recv2, self.send3, self.recv3 = [
+            sems.at[i] for i in range(8)
         ]
         self.rows = self.into.shape[1]
         self.decays = self.everything if decays is None else decays
@@ -199,28 +199,43 @@
                 decay = jnp.broadcast_to(self.decays[at, rows : rows + 1, :], (rows, LANES))
                 before = decay * before + self.everything[at, 0:rows, :]
 
-            def copy(chip, core):
+            def copy(chip):
                 return pltpu.make_async_remote_copy(
                     src_ref=self.found.at[chip],
                     dst_ref=self.into.at[self.z],
-                    send_sem=self.send3 if core else self.send2,
+                    send_sem=self.send2,
                     recv_sem=self.recv2,
-                    device_id={"ctx": 2 * chip + core},
+                    device_id={"ctx": 2 * chip + self.near},
                     device_id_type=MESH,
                 )
 
             def to(i, carry):
-                chip = far_first(self.z, i, count)
-                copy(chip, 0).start()
-                copy(chip, 1).start()
+                copy(far_first(self.z, i, count)).start()
                 return carry
 
             lax.fori_loop(0, count - 1, to, 0)
-            copy(self.z, 1).start()
-            pltpu.make_async_copy(self.found.at[self.z], self.into.at[self.z], self.recv2).start()
+            if self.near == 1:
+                copy(self.z).start()
+            else:
+                pltpu.make_async_copy(self.found.at[self.z], self.into.at[self.z], self.recv2).start()
 
     def result(self):
-        wait_bytes(self.into, self.recv2)
+        @pl.when(self.core == self.near)
+        def _():
+            wait_bytes(self.into, self.recv2)
+            pltpu.make_async_remote_copy(
+                src_ref=self.into,
+                dst_ref=self.into,
+                send_sem=self.send3,
+                recv_sem=self.recv3,
+                device_id={"ctx": 2 * self.z + 1 - self.near},
+                device_id_type=MESH,
+            ).start()
+
+        @pl.when(self.core != self.near)
+        def _():
+            wait_bytes(self.into, self.recv3)
+
         halves = []
         for half in range(2):
             at = pl.ds(half * self.chips // 2, self.chips // 2)
@@ -234,6 +249,7 @@
         @pl.when(self.core == self.near)
         def _():
             wait_bytes(self.start, self.peer_send)
+            wait_bytes(self.into, self.send3)
 
         @pl.when(self.core != self.near)
         def _():
@@ -241,8 +257,7 @@
 
         @pl.when(self.core == 0)
         def _():
-            wait_bytes(self.found.at[pl.ds(0, self.chips - 1)], self.send2)
-            wait_bytes(self.found, self.send3)
+            wait_bytes(self.found.at[pl.ds(0, self.chips - 1 + self.near)], self.send2)
 
 
 class Total:
@@ -254,8 +269,8 @@
     def send(self, value):
         self.part[...] = value.reshape(self.part.shape)
 
-        def to(k, carry):
-            there = lax.rem(self.tp + k, self.peers)
+        def to(i, carry):
+            there = far_first(self.tp, i, self.peers)
             pltpu.make_async_remote_copy(
                 src_ref=self.part.at[there],
                 dst_ref=self.taken.at[self.tp],
@@ -266,7 +281,7 @@
             ).start()
             return carry
 
-        lax.fori_loop(1, self.peers, to, 0)
+        lax.fori_loop(0, self.peers - 1, to, 0)
         pltpu.make_async_copy(self.part.at[self.tp], self.taken.at[self.tp], self.recv1).start()
 
     def add(self):
@@ -276,8 +291,8 @@
             total = total + self.taken[k]
         self.share[...] = total
 
-        def to(k, carry):
-            there = lax.rem(self.tp + k, self.peers)
+        def to(i, carry):
+            there = far_first(self.tp, i, self.peers)
             pltpu.make_async_remote_copy(
                 src_ref=self.share,
                 dst_ref=self.full.at[self.tp],
@@ -288,7 +303,7 @@
             ).start()
             return carry
 
-        lax.fori_loop(1, self.peers, to, 0)
+        lax.fori_loop(0, self.peers - 1, to, 0)
         pltpu.make_async_copy(self.share, self.full.at[self.tp], self.recv2).start()
 
     def result(self):
@@ -301,67 +316,87 @@
 
 
 class Columns:
-    def __init__(self, chips, peers, ctx, z, core, tp, inputs, cols, sems):
-        self.devices, self.peers = 2 * chips, peers
-        self.ctx, self.z, self.core, self.tp = ctx, z, core, tp
-        self.inputs, self.cols = inputs, cols
-        self.send1, self.recv1, self.send2, self.recv2 = [sems.at[i] for i in range(4)]
+    def __init__(self, chips, peers, z, core, tp, inputs, stage, cols, sems):
+        self.chips, self.peers = chips, peers
+        self.z, self.core, self.tp = z, core, tp
+        self.inputs, self.stage, self.cols = inputs, stage, cols
+        self.send1, self.recv1, self.send2, self.recv2, self.send3, self.recv3 = [
+            sems.at[i] for i in range(6)
+        ]
         self.share = 2 * LANES // peers
         self.sender = lax.div(tp * self.share, LANES)
         self.row = pl.multiple_of(lax.rem(tp * self.share, LANES), self.share)
 
-    def block(self, device):
-        at = pl.multiple_of(device * LANES, LANES)
-        return self.inputs.at[pl.ds(self.row, self.share), pl.ds(at, LANES)]
-
     def send(self):
         @pl.when(self.core == self.sender)
         def _():
-            def to(k, carry):
-                there = lax.rem(self.ctx + k, self.devices)
+            def block(chip):
+                at = pl.multiple_of(chip * 2 * LANES, 2 * LANES)
+                return self.inputs.at[pl.ds(self.row, self.share), pl.ds(at, 2 * LANES)]
+
+            def to(i, carry):
+                chip = far_first(self.z, i, self.chips)
                 pltpu.make_async_remote_copy(
-                    src_ref=self.block(there),
-                    dst_ref=self.cols.at[self.z, self.tp],
+                    src_ref=block(chip),
+                    dst_ref=self.stage.at[self.z],
                     send_sem=self.send1,
                     recv_sem=self.recv1,
-                    device_id={"ctx": there},
+                    device_id={"ctx": 2 * chip + self.core},
                     device_id_type=MESH,
                 ).start()
                 return carry
 
-            lax.fori_loop(1, self.devices, to, 0)
-            pltpu.make_async_copy(
-                self.block(self.ctx), self.cols.at[self.z, self.tp], self.recv1
+            lax.fori_loop(0, self.chips - 1, to, 0)
+            pltpu.make_async_copy(block(self.z), self.stage.at[self.z], self.recv1).start()
+
+    def share_out(self):
+        @pl.when(self.core == self.sender)
+        def _():
+            wait_bytes(self.stage, self.recv1)
+
+            def half(core):
+                at = pl.multiple_of(core * LANES, LANES)
+                return self.stage.at[:, :, pl.ds(at, LANES)]
+
+            pltpu.make_async_remote_copy(
+                src_ref=half(1 - self.core),
+                dst_ref=self.cols.at[:, self.tp],
+                send_sem=self.send2,
+                recv_sem=self.recv2,
+                device_id={"ctx": 2 * self.z + 1 - self.core},
+                device_id_type=MESH,
             ).start()
+            pltpu.make_async_copy(half(self.core), self.cols.at[:, self.tp], self.recv2).start()
 
     def spread(self):
         mine = self.cols.at[:, self.tp]
-        wait_bytes(mine, self.recv1)
-
-        def to(k, carry):
-            there = lax.rem(self.tp + k, self.peers)
+        wait_bytes(mine, self.recv2)
+
+        def to(i, carry):
+            there = far_first(self.tp, i, self.peers)
             pltpu.make_async_remote_copy(
                 src_ref=mine,
                 dst_ref=mine,
-                send_sem=self.send2,
-                recv_sem=self.recv2,
+                send_sem=self.send3,
+                recv_sem=self.recv3,
                 device_id={"tp": there},
                 device_id_type=MESH,
             ).start()
             return carry
 
-        lax.fori_loop(1, self.peers, to, 0)
+        lax.fori_loop(0, self.peers - 1, to, 0)
 
     def arrived(self):
-        wait_bytes(self.cols.at[:, pl.ds(0, self.peers - 1)], self.recv2)
+        wait_bytes(self.cols.at[:, pl.ds(0, self.peers - 1)], self.recv3)
 
     def finish(self):
         @pl.when(self.core == self.sender)
         def _():
-            sent = self.inputs.at[pl.ds(0, self.share), pl.ds(0, (self.devices - 1) * LANES)]
+            sent = self.inputs.at[pl.ds(0, self.share), pl.ds(0, (self.chips - 1) * 2 * LANES)]
             wait_bytes(sent, self.send1)
-
-        wait_bytes(self.cols.at[:, pl.ds(0, self.peers - 1)], self.send2)
+            wait_bytes(self.cols.at[:, self.tp], self.send2)
+
+        wait_bytes(self.cols.at[:, pl.ds(0, self.peers - 1)], self.send3)
 
 
 def kernel(
@@ -369,12 +404,12 @@
     inputs_hbm, w_hbm, b_hbm, c_hbm, ld_hbm, skip, dout_hbm,
     dw_ref, db_ref, dc_ref,
     inputs, b_ref, c_ref, ld_ref, dout_ref,
-    gw, gg, cols,
+    gw, gg, stage, cols,
     a_start, a_peer, a_joined, a_all, a_found, a_into,
     s_start, s_peer, s_joined, s_all, s_found, s_into,
     b_part, b_taken, b_share, b_full,
     c_part, c_taken, c_share, c_full,
-    ring_send, ring_recv, sib_recv, carry_sems, total_sems, cols_sems, fetch_sems,
+    ring_send, ring_recv, sib_recv, carry_sems, total_sems, cols_sems, fetch_sems, wave_sems,
 ):
     ctx, tp = lax.axis_index("ctx"), lax.axis_index("tp")
     devices = 2 * chips
@@ -399,20 +434,21 @@
 
     barrier = pltpu.get_barrier_semaphore()
 
-    def greet_ctx(k, carry):
-        pl.semaphore_signal(
-            barrier, inc=1, device_id={"ctx": lax.rem(ctx + k, devices)}, device_id_type=MESH
-        )
-        return carry
-
-    def greet_tp(k, carry):
-        pl.semaphore_signal(
-            barrier, inc=1, device_id={"tp": lax.rem(tp + k, peers)}, device_id_type=MESH
-        )
-        return carry
-
-    lax.fori_loop(1, devices, greet_ctx, 0)
-    lax.fori_loop(1, peers, greet_tp, 0)
+    near_chips = [k % chips for k in (1, -1, 2, -2)]
+    side = 4 if peers == 16 else 1
+    rest = peers // side
+    row, place = lax.div(tp, rest), lax.rem(tp, rest)
+    in_row = [row * rest + lax.rem(place + k, rest) for k in range(1, rest)]
+    in_column = [lax.rem(row + k, side) * rest + place for k in range(1, side)]
+    near = [{"ctx": 2 * lax.rem(z + k, chips) + c} for k in near_chips for c in range(2)]
+    near += [{"ctx": 2 * z + 1 - core}] + [{"tp": t} for t in in_row + in_column]
+
+    def greet(sem, who):
+        for device in who:
+            pl.semaphore_signal(sem, inc=1, device_id=device, device_id_type=MESH)
+        return len(who)
+
+    greeted = greet(barrier, near)
 
     ring_w = Ring(
         chips, 2, z, core, gw, ring_send.at[0], ring_send.at[1], ring_recv.at[0], sib_recv.at[0]
@@ -427,7 +463,7 @@
         chips, z, core, 0, a_all, (s_start, s_peer, s_joined, s_all, s_found, s_into), carry_sems.at[1]
     )
     total_b = Total(peers, tp, b_part, b_taken, b_share, b_full, total_sems.at[0])
-    columns = Columns(chips, peers, ctx, z, core, tp, inputs, cols, cols_sems)
+    columns = Columns(chips, peers, z, core, tp, inputs, stage, cols, cols_sems)
     total_c = Total(peers, tp, c_part, c_taken, c_share, c_full, total_sems.at[1])
 
     rows = lax.broadcasted_iota(jnp.int32, (LANES, LANES), 0)
@@ -452,16 +488,25 @@
     started = split(from_start * dout_wide)
     adjoint.put(dot_split(c_t, started), block_decay)
 
-    pl.semaphore_wait(barrier, devices - 1 + peers - 1)
-    for fetch in fetches[4:]:
-        fetch.wait()
+    fetches[4].wait()
+    pl.semaphore_wait(barrier, greeted)
 
     ring_w.begin()
     adjoint.hand()
-    adjoint.send()
+
+    met_row = greet(wave_sems.at[0], [{"tp": t} for t in in_row])
+    reach = 2
+    while 2 * reach <= chips // 2:
+        at = wave_sems.at[1 if reach == 2 else 2]
+        met = greet(at, [{"ctx": 2 * lax.rem(z + k, chips) + core} for k in (reach, chips - reach)])
+        pl.semaphore_wait(at, met)
+        reach *= 2
+    pl.semaphore_wait(wave_sems.at[0], met_row)
+    fetches[5].wait()
+
     ring_w.step(2)
     ring_w.step(1)
-    columns.send()
+    adjoint.send()
 
     def project(total, chip):
         at = pl.multiple_of(chip * 2 * LANES, 2 * LANES)
@@ -470,15 +515,16 @@
 
     ring_w.step(4)
     ring_w.step(3)
+    columns.send()
     ring_w.arrived(0)
     projected = project(jnp.zeros((LANES, 2 * LANES), F32), z)
     for k in (1, 2):
         projected = project(projected, ring_w.source(k))
         ring_w.arrived(k)
         projected = project(projected, ring_w.sibling_source(k))
-    adjoint.work()
     ring_w.step(6)
     ring_w.step(5)
+    adjoint.work()
 
     scores_t = dot(b, c, SECOND_T)
     later = lanes >= rows
@@ -497,7 +543,7 @@
         local.append(jnp.where(first, sides[0], sides[1]) + scale * pair.astype(F32))
     local = jnp.concatenate(local, axis=1)
 
-    columns.spread()
+    columns.share_out()
     for k in range(3, chips // 2 - 1):
         projected = project(projected, ring_w.source(k))
         ring_w.arrived(k)
@@ -515,12 +561,12 @@
     ended = split(to_end * values.astype(F32))
     state.put(dot_split(b_t, ended), block_decay)
     state.hand()
-
+    columns.spread()
+    state.send()
     adjoint_in = adjoint.result()
     grad_values = local + to_end * dot_split(b, adjoint_in)
     gg[ctx] = grad_values.astype(BF16)
     ring_g.begin()
-    state.send()
 
     d_b = carried(ended, adjoint_in)
     d_c = jnp.zeros((LANES, LANES), F32)
@@ -537,33 +583,39 @@
     total_b.send(d_b)
     ring_g.step(2)
     ring_g.step(1)
+
+    def project_back(total, chip):
+        return total + dot(
+            cols[chip].reshape(2 * LANES, LANES).astype(F32).T.astype(BF16),
+            gg[pl.ds(2 * chip, 2)].reshape(2 * LANES, -1),
+        )
+
+    columns.arrived()
+    ring_g.arrived(0)
+    grad_w = project_back(jnp.zeros((LANES, 2 * LANES), F32), z)
     ring_g.step(4)
     ring_g.step(3)
     state.work()
     total_b.add()
+
+    def back_both(total, k):
+        total = project_back(total, ring_g.source(k))
+        ring_g.arrived(k)
+        return project_back(total, ring_g.sibling_source(k))
+
+    for k in (1, 2):
+        grad_w = back_both(grad_w, k)
     ring_g.step(6)
     ring_g.step(5)
     state_in = state.result()
     d_c = d_c + carried(started, state_in)
     total_c.send(d_c)
+    for k in range(3, chips // 2 - 1):
+        grad_w = back_both(grad_w, k)
     ring_g.step(8)
     ring_g.step(7)
     total_c.add()
-
-    columns.arrived()
-
-    def project_back(total, chip):
-        return total + dot(
-            cols[chip].reshape(2 * LANES, LANES).astype(F32).T.astype(BF16),
-            gg[pl.ds(2 * chip, 2)].reshape(2 * LANES, -1),
-        )
-
-    ring_g.arrived(0)
-    grad_w = project_back(jnp.zeros((LANES, 2 * LANES), F32), z)
-    for k in range(1, chips // 2):
-        grad_w = project_back(grad_w, ring_g.source(k))
-        ring_g.arrived(k)
-        grad_w = project_back(grad_w, ring_g.sibling_source(k))
+    grad_w = back_both(grad_w, chips // 2 - 1)
     ring_g.arrived(chips // 2)
     dw_ref[...] = project_back(grad_w, ring_g.source(chips // 2))
     db_ref[...] = total_b.result()
@@ -620,6 +672,7 @@
                 pltpu.VMEM(d_out.shape, BF16),
                 pltpu.VMEM((devices, tokens, width), BF16),
                 pltpu.VMEM((devices, tokens, width), BF16),
+                pltpu.VMEM((chips, 2 * tokens // peers, 2 * LANES), BF16),
                 pltpu.VMEM((chips, peers, 2 * tokens // peers, LANES), BF16),
             ]
             + carry_scratch(rows + 8)
@@ -629,10 +682,11 @@
                 pltpu.SemaphoreType.DMA((4,)),
                 pltpu.SemaphoreType.DMA((2, half + 1, 2)),
                 pltpu.SemaphoreType.DMA((2, half + 1, 2)),
-                pltpu.SemaphoreType.DMA((2, 7)),
+                pltpu.SemaphoreType.DMA((2, 8)),
                 pltpu.SemaphoreType.DMA((2, 4)),
-                pltpu.SemaphoreType.DMA((4,)),
                 pltpu.SemaphoreType.DMA((6,)),
+                pltpu.SemaphoreType.DMA((6,)),
+                pltpu.SemaphoreType.REGULAR((3,)),
             ],
             compiler_params=pltpu.CompilerParams(
                 collective_id=0, has_side_effects=True, vmem_limit_bytes=60 * 1024 * 1024

time: 84.7 us -> 87.4 us (1.032)
  Pallas kernels: 80.7 us -> 83.5 us
    pallas_call x1, Pallas kernels: 80.7 us -> 83.5 us  [per_device(): pl.pallas_call(functools.partial(kernel, chips, peers), out_shape=(jax.Sh...]
where the time goes in v3:
time: 87.4 us; the launch traced here: 87.2 us
  Pallas kernels  83.5 us (96%)
  local copies, waits for them, and re-layouts  3.09 us (4%)
    pallas_call x1, Pallas kernels, per_device(): pl.pallas_call(functools.partial(kernel, chips, peers), out_shape=(jax.Sh...  83.5 us
    unnamed x7, local copies, waits for them, and re-layouts  3.09 us

profile of v3, /device:TPU:1, one launch (start us, length us, event | category | flops | bytes accessed | tf_op | source)
XLA Modules:
  0.0 87.2 jit_solution(15617291030324338103)
XLA Ops:
  0.6 83.5 %shard_map.94 = (f32[128,256]{1,0:T(8,128)}, f32[128,128]{1,0:T(8,128)}, f32[128,128]{1,0:T(8,128)}) custom-call(bf16[128,4096]{1,0:T(8,128)(2,1)} %inputs_hbm.1, bf16[128,256]{1,0:T(8,128)(2,1)} %w_hbm.1, bf16[128,128]{1,0:T(8,128)(2,1)} %b_hbm.1, bf16[128,128]{1,0:T(8,128)(2,1)} %c_hbm.1, f32[4,128]{1,0:T(4,128)} %bitcast.1, f32[4]{0:T(128)} %skip.1, ...), custom_call_target="tpu_custom_call" | custom-call | tf_op jit(solution)/shard_map/pallas_call | solution.py:658
  84.1 0.0 copy-start.1
  84.1 1.6 %copy.13 = f32[128,256]{1,0:T(8,128)} copy(f32[128,256]{1,0:T(8,128)} %get-tuple-element.6) | data formatting | bytes 262144
  85.7 0.0 copy-done.1
  85.7 0.0 copy-start
  85.7 0.6 copy.14
  86.3 0.2 copy-done
  86.6 0.6 copy.15
Async XLA Ops:
  84.1 1.6 %copy-start.1 = (f32[128,128]{1,0:T(8,128)S(1)}, f32[128,128]{1,0:T(8,128)}, u32[]{:S(2)}) copy-start(f32[128,128]{1,0:T(8,128)} %get-tuple-element.7) | copy-start | bytes 196612
  85.7 0.9 copy-start

commit v4 on v3

--- a/solution.py
+++ b/solution.py
@@ -12,6 +12,7 @@
 MESH = pl.DeviceIdType.MESH
 HIGHEST = lax.Precision.HIGHEST
 LANES = 128
+RING_W, RING_G = ((2,), 2), ((2,), 2)
 PLAIN = ((1,), (0,))
 SECOND_T = ((1,), (1,))
 
@@ -43,22 +44,26 @@
 
 
 class Ring:
-    def __init__(self, chips, stride, z, core, blocks, ring_send, sib_send, ring_recv, sib_recv):
-        self.chips, self.stride, self.half = chips, stride, chips // 2
+    def __init__(self, chips, legs, parts, z, core, blocks, ring_send, sib_send, ring_recv, sib_recv):
+        self.chips, self.parts, self.half = chips, parts, chips // 2
+        self.leg, self.order, at = {}, [], 0
+        while at < self.half:
+            self.leg[at] = min(legs[len(self.leg) % len(legs)], self.half - at)
+            self.order += range(at + self.leg[at], at, -1)
+            at += self.leg[at]
         self.z, self.core, self.blocks = z, core, blocks
         self.ring_send, self.sib_send = ring_send, sib_send
         self.ring_recv, self.sib_recv = ring_recv, sib_recv
         self.sibling, self.mine = 2 * z + 1 - core, 2 * z + core
-
-    def copy(self, block, to, send, recv):
+        self.rows = blocks.shape[1] // parts
+
+    def copy(self, ref, to, send, recv):
         pltpu.make_async_remote_copy(
-            src_ref=self.blocks.at[block],
-            dst_ref=self.blocks.at[block],
-            send_sem=send,
-            recv_sem=recv,
-            device_id={"ctx": to},
-            device_id_type=MESH,
+            src_ref=ref, dst_ref=ref, send_sem=send, recv_sem=recv, device_id={"ctx": to}, device_id_type=MESH
         ).start()
+
+    def part(self, block, p):
+        return self.blocks.at[block, pl.ds(p * self.rows, self.rows)]
 
     def back(self, k):
         return lax.rem(self.z + (self.chips - k), self.chips)
@@ -72,41 +77,53 @@
     def sibling_source(self, k):
         return jnp.where(self.core == 0, self.ahead(k), self.back(k))
 
+    def onward(self, k):
+        return 2 * self.sibling_source(k) + self.core
+
     def begin(self):
-        for s in range(self.stride, 0, -1):
-            recv = self.ring_recv.at[s, self.core]
-            self.copy(self.mine, 2 * self.ahead(s), self.ring_send, recv)
-            self.copy(self.mine, 2 * self.back(s) + 1, self.ring_send, recv)
-        self.copy(self.mine, self.sibling, self.sib_send, self.sib_recv.at[0, 0])
+        leg = self.leg[0]
+        for p in range(self.parts):
+            recv = self.ring_recv.at[leg, self.core * self.parts + p]
+            self.copy(self.part(self.mine, p), 2 * self.ahead(leg), self.ring_send, recv)
+            self.copy(self.part(self.mine, p), 2 * self.back(leg) + 1, self.ring_send, recv)
+        for s in range(leg - 1, 0, -1):
+            recv = self.ring_recv.at[s, 0]
+            self.copy(self.blocks.at[self.mine], 2 * self.ahead(s), self.ring_send, recv)
+            self.copy(self.blocks.at[self.mine], 2 * self.back(s) + 1, self.ring_send, recv)
+        self.copy(self.blocks.at[self.mine], self.sibling, self.sib_send, self.sib_recv.at[0])
 
     def step(self, k):
-        if k > self.half:
-            return
         base = 2 * self.source(k)
+        whole = self.blocks.at[base + self.core if k == self.half else pl.ds(base, 2)]
         if k == self.half:
-            block = base + self.core
-            wait_bytes(self.blocks.at[block], self.ring_recv.at[k, 0])
-            self.copy(block, self.sibling, self.sib_send, self.sib_recv.at[k, 0])
-            return
-        onward = [s for s in range(self.stride, 0, -1) if k % self.stride == 0 and k + s <= self.half]
-        for h in range(2):
-            wait_bytes(self.blocks.at[base + h], self.ring_recv.at[k, h])
-            for s in onward:
-                if k + s < self.half:
-                    to = 2 * self.sibling_source(s) + self.core
-                    self.copy(base + h, to, self.ring_send, self.ring_recv.at[k + s, h])
-            self.copy(base + h, self.sibling, self.sib_send, self.sib_recv.at[k, h])
-        for s in onward:
-            if k + s == self.half:
-                to = 2 * self.sibling_source(s) + self.core
-                self.copy(base + self.core, to, self.ring_send, self.ring_recv.at[k + s, 0])
+            for p in range(self.parts):
+                wait_bytes(self.part(base + self.core, p), self.ring_recv.at[k, p])
+        elif k not in self.leg:
+            wait_bytes(whole, self.ring_recv.at[k, 0])
+        else:
+            leg = self.leg[k]
+            there = k + leg
+            for p in range(self.parts):
+                for h in range(2):
+                    at = h * self.parts + p
+                    wait_bytes(self.part(base + h, p), self.ring_recv.at[k, at])
+                    if there < self.half:
+                        recv = self.ring_recv.at[there, at]
+                        self.copy(self.part(base + h, p), self.onward(leg), self.ring_send, recv)
+                if there == self.half:
+                    recv = self.ring_recv.at[there, p]
+                    self.copy(self.part(base + self.core, p), self.onward(leg), self.ring_send, recv)
+            for s in range(leg - 1, 0, -1):
+                self.copy(whole, self.onward(s), self.ring_send, self.ring_recv.at[k + s, 0])
+        self.copy(whole, self.sibling, self.sib_send, self.sib_recv.at[k])
+
+    def steps(self, *ks):
+        for k in sorted((k for k in ks if k <= self.half), key=self.order.index):
+            self.step(k)
 
     def arrived(self, k):
-        if k == 0 or k == self.half:
-            wait_bytes(self.blocks.at[0], self.sib_recv.at[k, 0])
-        else:
-            for h in range(2):
-                wait_bytes(self.blocks.at[h], self.sib_recv.at[k, h])
+        got = self.blocks.at[pl.ds(0, 1 if k == 0 or k == self.half else 2)]
+        wait_bytes(got, self.sib_recv.at[k])
 
     def finish(self):
         wait_bytes(self.blocks.at[pl.ds(0, self.chips - 1)], self.ring_send)
@@ -122,7 +139,7 @@
         ]
         self.rows = self.into.shape[1]
         self.decays = self.everything if decays is None else decays
-        self.sent = self.everything.shape[1]
+        self.sent = self.rows + (decays is None)
 
     def put(self, state, decay):
         slices, rows = self.chips, self.rows
@@ -160,7 +177,7 @@
             def copy(chip):
                 return dict(
                     src_ref=self.joined.at[chip, pl.ds(0, self.sent)],
-                    dst_ref=self.everything.at[self.z],
+                    dst_ref=self.everything.at[self.z, pl.ds(0, self.sent)],
                 )
 
             def to(i, carry):
@@ -191,7 +208,7 @@
 
         @pl.when(self.core == 0)
         def _():
-            wait_bytes(self.everything, self.recv1)
+            wait_bytes(self.everything.at[:, pl.ds(0, self.sent)], self.recv1)
             before = jnp.zeros((rows, LANES), F32)
             for k in range(count):
                 at = count - 1 - k if self.near == 1 else k
@@ -451,10 +468,10 @@
     greeted = greet(barrier, near)
 
     ring_w = Ring(
-        chips, 2, z, core, gw, ring_send.at[0], ring_send.at[1], ring_recv.at[0], sib_recv.at[0]
+        chips, *RING_W, z, core, gw, ring_send.at[0], ring_send.at[1], ring_recv.at[0], sib_recv.at[0]
     )
     ring_g = Ring(
-        chips, 2, z, core, gg, ring_send.at[2], ring_send.at[3], ring_recv.at[1], sib_recv.at[1]
+        chips, *RING_G, z, core, gg, ring_send.at[2], ring_send.at[3], ring_recv.at[1], sib_recv.at[1]
     )
     adjoint = Carry(
         chips, z, core, 1, None, (a_start, a_peer, a_joined, a_all, a_found, a_into), carry_sems.at[0]
@@ -504,27 +521,19 @@
     pl.semaphore_wait(wave_sems.at[0], met_row)
     fetches[5].wait()
 
-    ring_w.step(2)
-    ring_w.step(1)
     adjoint.send()
+    ring_w.steps(1, 2)
+    columns.send()
 
     def project(total, chip):
         at = pl.multiple_of(chip * 2 * LANES, 2 * LANES)
         block = gw[pl.ds(2 * chip, 2)].reshape(2 * LANES, -1)
         return total + dot(inputs[:, pl.ds(at, 2 * LANES)], block)
 
-    ring_w.step(4)
-    ring_w.step(3)
-    columns.send()
-    ring_w.arrived(0)
-    projected = project(jnp.zeros((LANES, 2 * LANES), F32), z)
-    for k in (1, 2):
-        projected = project(projected, ring_w.source(k))
+    def project_both(total, k):
+        total = project(total, ring_w.source(k))
         ring_w.arrived(k)
-        projected = project(projected, ring_w.sibling_source(k))
-    ring_w.step(6)
-    ring_w.step(5)
-    adjoint.work()
+        return project(total, ring_w.sibling_source(k))
 
     scores_t = dot(b, c, SECOND_T)
     later = lanes >= rows
@@ -543,26 +552,28 @@
         local.append(jnp.where(first, sides[0], sides[1]) + scale * pair.astype(F32))
     local = jnp.concatenate(local, axis=1)
 
+    ring_w.steps(3, 4)
+    ring_w.arrived(0)
+    projected = project(jnp.zeros((LANES, 2 * LANES), F32), z)
+    for k in (1, 2):
+        projected = project_both(projected, k)
+    ring_w.steps(5, 6)
+    adjoint.work()
     columns.share_out()
     for k in range(3, chips // 2 - 1):
-        projected = project(projected, ring_w.source(k))
-        ring_w.arrived(k)
-        projected = project(projected, ring_w.sibling_source(k))
-    ring_w.step(8)
-    ring_w.step(7)
-
-    k = chips // 2 - 1
-    projected = project(projected, ring_w.source(k))
-    ring_w.arrived(k)
-    projected = project(projected, ring_w.sibling_source(k))
+        projected = project_both(projected, k)
+    columns.spread()
+    ring_w.steps(7, 8)
+
+    projected = project_both(projected, chips // 2 - 1)
     ring_w.arrived(chips // 2)
     projected = project(projected, ring_w.source(chips // 2))
     values = projected.astype(BF16)
     ended = split(to_end * values.astype(F32))
     state.put(dot_split(b_t, ended), block_decay)
     state.hand()
-    columns.spread()
     state.send()
+
     adjoint_in = adjoint.result()
     grad_values = local + to_end * dot_split(b, adjoint_in)
     gg[ctx] = grad_values.astype(BF16)
@@ -581,8 +592,14 @@
         d_c = d_c + dot(weights, b)
         d_b = d_b + dot(weights_t, c)
     total_b.send(d_b)
-    ring_g.step(2)
-    ring_g.step(1)
+    ring_g.steps(1, 2)
+    state.work()
+    ring_g.steps(3, 4)
+    total_b.add()
+    ring_g.steps(5, 6)
+    state_in = state.result()
+    d_c = d_c + carried(started, state_in)
+    total_c.send(d_c)
 
     def project_back(total, chip):
         return total + dot(
@@ -590,30 +607,17 @@
             gg[pl.ds(2 * chip, 2)].reshape(2 * LANES, -1),
         )
 
-    columns.arrived()
-    ring_g.arrived(0)
-    grad_w = project_back(jnp.zeros((LANES, 2 * LANES), F32), z)
-    ring_g.step(4)
-    ring_g.step(3)
-    state.work()
-    total_b.add()
-
     def back_both(total, k):
         total = project_back(total, ring_g.source(k))
         ring_g.arrived(k)
         return project_back(total, ring_g.sibling_source(k))
 
-    for k in (1, 2):
+    columns.arrived()
+    ring_g.arrived(0)
+    grad_w = project_back(jnp.zeros((LANES, 2 * LANES), F32), z)
+    ring_g.steps(7, 8)
+    for k in range(1, chips // 2 - 1):
         grad_w = back_both(grad_w, k)
-    ring_g.step(6)
-    ring_g.step(5)
-    state_in = state.result()
-    d_c = d_c + carried(started, state_in)
-    total_c.send(d_c)
-    for k in range(3, chips // 2 - 1):
-        grad_w = back_both(grad_w, k)
-    ring_g.step(8)
-    ring_g.step(7)
     total_c.add()
     grad_w = back_both(grad_w, chips // 2 - 1)
     ring_g.arrived(chips // 2)
@@ -680,8 +684,8 @@
             + total_scratch * 2
             + [
                 pltpu.SemaphoreType.DMA((4,)),
-                pltpu.SemaphoreType.DMA((2, half + 1, 2)),
-                pltpu.SemaphoreType.DMA((2, half + 1, 2)),
+                pltpu.SemaphoreType.DMA((2, half + 1, 2 * max(RING_W[1], RING_G[1]))),
+                pltpu.SemaphoreType.DMA((2, half + 1)),
                 pltpu.SemaphoreType.DMA((2, 8)),
                 pltpu.SemaphoreType.DMA((2, 4)),
                 pltpu.SemaphoreType.DMA((6,)),

time: 87.4 us -> 78.6 us (0.90)
  Pallas kernels: 83.5 us -> 74.7 us
    pallas_call x1, Pallas kernels: 83.5 us -> 74.7 us  [per_device(): pl.pallas_call(functools.partial(kernel, chips, peers), out_shape=(jax.Sh...]
where the time goes in v4:
time: 78.6 us; the launch traced here: 78.4 us
  Pallas kernels  74.7 us (95%)
  local copies, waits for them, and re-layouts  3.09 us (4%)
    pallas_call x1, Pallas kernels, per_device(): pl.pallas_call(functools.partial(kernel, chips, peers), out_shape=(jax.Sh...  74.7 us
    unnamed x7, local copies, waits for them, and re-layouts  3.09 us

profile of v4, /device:TPU:1, one launch (start us, length us, event | category | flops | bytes accessed | tf_op | source)
XLA Modules:
  0.0 78.4 jit_solution(14872375931383750136)
XLA Ops:
  0.6 74.7 %shard_map.94 = (f32[128,256]{1,0:T(8,128)}, f32[128,128]{1,0:T(8,128)}, f32[128,128]{1,0:T(8,128)}) custom-call(bf16[128,4096]{1,0:T(8,128)(2,1)} %inputs_hbm.1, bf16[128,256]{1,0:T(8,128)(2,1)} %w_hbm.1, bf16[128,128]{1,0:T(8,128)(2,1)} %b_hbm.1, bf16[128,128]{1,0:T(8,128)(2,1)} %c_hbm.1, f32[4,128]{1,0:T(4,128)} %bitcast.1, f32[4]{0:T(128)} %skip.1, ...), custom_call_target="tpu_custom_call" | custom-call | tf_op jit(solution)/shard_map/pallas_call | solution.py:662
  75.3 0.0 copy-start.1
  75.3 1.6 %copy.13 = f32[128,256]{1,0:T(8,128)} copy(f32[128,256]{1,0:T(8,128)} %get-tuple-element.6) | data formatting | bytes 262144
  76.9 0.0 copy-done.1
  76.9 0.0 copy-start
  76.9 0.6 copy.14
  77.6 0.2 copy-done
  77.8 0.6 copy.15
Async XLA Ops:
  75.3 1.6 %copy-start.1 = (f32[128,128]{1,0:T(8,128)S(1)}, f32[128,128]{1,0:T(8,128)}, u32[]{:S(2)}) copy-start(f32[128,128]{1,0:T(8,128)} %get-tuple-element.7) | copy-start | bytes 196612
  76.9 0.9 %copy-start = (f32[128,128]{1,0:T(8,128)S(1)}, f32[128,128]{1,0:T(8,128)}, u32[]{:S(2)}) copy-start(f32[128,128]{1,0:T(8,128)} %get-tuple-element.8) | copy-start | bytes 196612

commit v5 on v4

--- a/solution.py
+++ b/solution.py
@@ -433,22 +433,6 @@
     z, core = lax.div(ctx, 2), lax.rem(ctx, 2)
     heads = 4
 
-    fetches = [
-        pltpu.make_async_copy(there, here, fetch_sems.at[i])
-        for i, (there, here) in enumerate(
-            [
-                (ld_hbm, ld_ref),
-                (c_hbm, c_ref),
-                (dout_hbm, dout_ref),
-                (b_hbm, b_ref),
-                (w_hbm, gw.at[ctx]),
-                (inputs_hbm, inputs),
-            ]
-        )
-    ]
-    for fetch in fetches:
-        fetch.start()
-
     barrier = pltpu.get_barrier_semaphore()
 
     near_chips = [k % chips for k in (1, -1, 2, -2)]
@@ -466,6 +450,21 @@
         return len(who)
 
     greeted = greet(barrier, near)
+    fetches = [
+        pltpu.make_async_copy(there, here, fetch_sems.at[i])
+        for i, (there, here) in enumerate(
+            [
+                (w_hbm, gw.at[ctx]),
+                (ld_hbm, ld_ref),
+                (c_hbm, c_ref),
+                (dout_hbm, dout_ref),
+                (b_hbm, b_ref),
+                (inputs_hbm, inputs),
+            ]
+        )
+    ]
+    for fetch in fetches:
+        fetch.start()
 
     ring_w = Ring(
         chips, *RING_W, z, core, gw, ring_send.at[0], ring_send.at[1], ring_recv.at[0], sib_recv.at[0]
@@ -483,17 +482,32 @@
     columns = Columns(chips, peers, z, core, tp, inputs, stage, cols, cols_sems)
     total_c = Total(peers, tp, c_part, c_taken, c_share, c_full, total_sems.at[1])
 
+    fetches[0].wait()
+    pl.semaphore_wait(barrier, greeted)
+    ring_w.begin()
+
+    met_row = greet(wave_sems.at[0], [{"tp": t} for t in in_row])
+
+    def vouch(reach):
+        at = wave_sems.at[1 if reach == 2 else 2]
+        return at, greet(at, [{"ctx": 2 * lax.rem(z + k, chips) + core} for k in (reach, chips - reach)])
+
+    met = vouch(2)
+
     rows = lax.broadcasted_iota(jnp.int32, (LANES, LANES), 0)
     lanes = lax.broadcasted_iota(jnp.int32, (LANES, LANES), 1)
     upper = (rows <= lanes).astype(F32)
     first, first_rows = lanes < LANES // 2, rows < LANES // 2
-    for fetch in fetches[:4]:
+    for fetch in fetches[1:5]:
         fetch.wait()
     cumulative_t = []
     for q in range(2):
         pair = [jnp.broadcast_to(ld_ref[2 * q + i : 2 * q + i + 1, :], (LANES, LANES)) for i in range(2)]
         cumulative_t.append(dot(jnp.where(first_rows, pair[0], pair[1]), upper, precision=HIGHEST))
     cumulative = jnp.concatenate([part.T for part in cumulative_t], axis=1)
+    pl.semaphore_wait(*met)
+    if chips > 8:
+        met = vouch(4)
     block_log = cumulative[LANES - 1 : LANES, :]
     block_decay = jnp.exp(block_log)
     to_end = jnp.exp(block_log - cumulative)
@@ -505,22 +519,11 @@
     started = split(from_start * dout_wide)
     adjoint.put(dot_split(c_t, started), block_decay)
 
-    fetches[4].wait()
-    pl.semaphore_wait(barrier, greeted)
-
-    ring_w.begin()
     adjoint.hand()
-
-    met_row = greet(wave_sems.at[0], [{"tp": t} for t in in_row])
-    reach = 2
-    while 2 * reach <= chips // 2:
-        at = wave_sems.at[1 if reach == 2 else 2]
-        met = greet(at, [{"ctx": 2 * lax.rem(z + k, chips) + core} for k in (reach, chips - reach)])
-        pl.semaphore_wait(at, met)
-        reach *= 2
+    if chips > 8:
+        pl.semaphore_wait(*met)
     pl.semaphore_wait(wave_sems.at[0], met_row)
     fetches[5].wait()
-
     adjoint.send()
     ring_w.steps(1, 2)
     columns.send()
@@ -662,9 +665,9 @@
         return pl.pallas_call(
             functools.partial(kernel, chips, peers),
             out_shape=(
-                jax.ShapeDtypeStruct(w_in.shape, F32),
-                jax.ShapeDtypeStruct(b_in.shape, F32),
-                jax.ShapeDtypeStruct(c_in.shape, F32),
+                pltpu.VMEM(w_in.shape, F32),
+                pltpu.VMEM(b_in.shape, F32),
+                pltpu.VMEM(c_in.shape, F32),
             ),
             in_specs=[hbm] * 5 + [pl.BlockSpec(memory_space=pltpu.SMEM), hbm],
             out_specs=(vmem, vmem, vmem),

time: 78.6 us -> 76.6 us (0.975)
  local copies, waits for them, and re-layouts: 3.09 us -> 1.92 us
  Pallas kernels: 74.7 us -> 73.9 us
    unnamed x7 -> x3, local copies, waits for them, and re-layouts: 3.09 us -> 1.92 us
where the time goes in v5:
time: 76.6 us; the launch traced here: 76.5 us
  Pallas kernels  73.9 us (96%)
  local copies, waits for them, and re-layouts  1.92 us (3%)
    pallas_call x1, Pallas kernels, per_device(): pl.pallas_call(functools.partial(kernel, chips, peers), out_shape=(pltpu....  73.9 us
    unnamed x3, local copies, waits for them, and re-layouts  1.92 us

profile of v5, /device:TPU:1, one launch (start us, length us, event | category | flops | bytes accessed | tf_op | source)
XLA Modules:
  0.0 76.5 jit_solution(9610815841871198615)
XLA Ops:
  0.6 73.9 %shard_map.94 = (f32[128,256]{1,0:T(8,128)S(1)}, f32[128,128]{1,0:T(8,128)S(1)}, f32[128,128]{1,0:T(8,128)S(1)}) custom-call(bf16[128,4096]{1,0:T(8,128)(2,1)} %inputs_hbm.1, bf16[128,256]{1,0:T(8,128)(2,1)} %w_hbm.1, bf16[128,128]{1,0:T(8,128)(2,1)} %b_hbm.1, bf16[128,128]{1,0:T(8,128)(2,1)} %c_hbm.1, f32[4,128]{1,0:T(4,128)} %bitcast.1, f32[4]{0:T(128)} %skip.1, ...), custom_call_target="tpu_custom_call" | custom-call | tf_op jit(solution)/shard_map/pallas_call | solution.py:665
  74.5 0.7 copy.13
  75.2 0.6 copy.14
  75.8 0.6 copy.15

commit v6 on v5

--- a/solution.py
+++ b/solution.py
@@ -171,8 +171,10 @@
         def _():
             wait_bytes(self.peer, self.peer_recv)
             decay = self.start[:, rows : rows + 1, :]
-            self.joined[:, pl.ds(0, rows), :] = self.start[:, 0:rows, :] + decay * self.peer[:, 0:rows, :]
-            self.joined[:, pl.ds(rows, 8), :] = decay * self.peer[:, rows : rows + 8, :]
+            both = self.start[:, 0:rows, :] + decay * self.peer[:, 0:rows, :]
+            self.joined[:, pl.ds(0, rows), :] = both.astype(self.joined.dtype)
+            if self.sent > rows:
+                self.joined[:, pl.ds(rows, 8), :] = decay * self.peer[:, rows : rows + 8, :]
 
             def copy(chip):
                 return dict(
@@ -214,7 +216,7 @@
                 at = count - 1 - k if self.near == 1 else k
                 self.found[at] = before.astype(BF16)
                 decay = jnp.broadcast_to(self.decays[at, rows : rows + 1, :], (rows, LANES))
-                before = decay * before + self.everything[at, 0:rows, :]
+                before = decay * before + self.everything[at, 0:rows, :].astype(F32)
 
             def copy(chip):
                 return pltpu.make_async_remote_copy(
@@ -595,8 +597,8 @@
         d_c = d_c + dot(weights, b)
         d_b = d_b + dot(weights_t, c)
     total_b.send(d_b)
+    state.work()
     ring_g.steps(1, 2)
-    state.work()
     ring_g.steps(3, 4)
     total_b.add()
     ring_g.steps(5, 6)
@@ -645,12 +647,12 @@
         tokens, width = d_out.shape
         rows = LANES // (chips // 2)
         vmem, hbm = pl.BlockSpec(memory_space=pltpu.VMEM), pl.BlockSpec(memory_space=pltpu.HBM)
-        def carry_scratch(sent):
+        def carry_scratch(sent, dtype):
             return [
                 pltpu.VMEM((chips, rows + 8, LANES), F32),
                 pltpu.VMEM((chips, rows + 8, LANES), F32),
-                pltpu.VMEM((chips, rows + 8, LANES), F32),
-                pltpu.VMEM((chips, sent, LANES), F32),
+                pltpu.VMEM((chips, sent, LANES), dtype),
+                pltpu.VMEM((chips, sent, LANES), dtype),
                 pltpu.VMEM((chips, rows, LANES), BF16),
                 pltpu.VMEM((chips, rows, LANES), BF16),
             ]
@@ -682,8 +684,8 @@
                 pltpu.VMEM((chips, 2 * tokens // peers, 2 * LANES), BF16),
                 pltpu.VMEM((chips, peers, 2 * tokens // peers, LANES), BF16),
             ]
-            + carry_scratch(rows + 8)
-            + carry_scratch(rows)
+            + carry_scratch(rows + 8, F32)
+            + carry_scratch(rows, BF16)
             + total_scratch * 2
             + [
                 pltpu.SemaphoreType.DMA((4,)),

time: 76.6 us -> 75.6 us (0.987)
  Pallas kernels: 73.9 us -> 72.9 us
    pallas_call x1, Pallas kernels: 73.9 us -> 72.9 us  [per_device(): pl.pallas_call(functools.partial(kernel, chips, peers), out_shape=(pltpu....]
where the time goes in v6:
time: 75.6 us; the launch traced here: 75.5 us
  Pallas kernels  72.9 us (96%)
  local copies, waits for them, and re-layouts  1.92 us (3%)
    pallas_call x1, Pallas kernels, per_device(): pl.pallas_call(functools.partial(kernel, chips, peers), out_shape=(pltpu....  72.9 us
    unnamed x3, local copies, waits for them, and re-layouts  1.92 us

profile of v6, /device:TPU:1, one launch (start us, length us, event | category | flops | bytes accessed | tf_op | source)
XLA Modules:
  0.0 75.5 jit_solution(11676219721022198081)
XLA Ops:
  0.6 72.9 %shard_map.94 = (f32[128,256]{1,0:T(8,128)S(1)}, f32[128,128]{1,0:T(8,128)S(1)}, f32[128,128]{1,0:T(8,128)S(1)}) custom-call(bf16[128,4096]{1,0:T(8,128)(2,1)} %inputs_hbm.1, bf16[128,256]{1,0:T(8,128)(2,1)} %w_hbm.1, bf16[128,128]{1,0:T(8,128)(2,1)} %b_hbm.1, bf16[128,128]{1,0:T(8,128)(2,1)} %c_hbm.1, f32[4,128]{1,0:T(4,128)} %bitcast.1, f32[4]{0:T(128)} %skip.1, ...), custom_call_target="tpu_custom_call" | custom-call | tf_op jit(solution)/shard_map/pallas_call | solution.py:667
  73.5 0.7 copy.13
  74.2 0.6 copy.14
  74.8 0.6 copy.15
